TPU v7x, 32 devices: a whole 2x2x4 slice. The times are simulated.
32 devices in a mesh: path: 8 (over z, y), tp: 4 (over x, core).
Axes of the slice: x: 2, y: 2, z: 4, core: 2. Of those that a mesh axis runs over, the one named last changes fastest.
Arguments:
- token_ids: int32 [8, 1024], P('path'), may hold values from 0 to 31999
- targets: int32 [8, 128], P('path'), may hold values from 0 to 31999
- loss_positions: int32 [8, 128], P('path'), may hold values from 0 to 1023
- doc_lengths: int32 [8, 8], P('path'), may hold values from 1 to 512, 1024 in all within a row
- live_tokens: int32 [8], P('path'), may hold values from 512 to 1024
- routes: int32 [8, 2], replicated, may hold values from 0 to 3, as said below
- attn_master: float32 [4, 896, 4096], P(None, 'path', 'tp'), may hold values from -0.25 to 0.25
- mlp_master: float32 [4, 896, 7168], P(None, 'path', 'tp'), may hold values from -0.1875 to 0.1875
- gain_master: float32 [4, 896, 2], P(None, 'path'), may hold values from 0.5 to 1.5
- table_master: float32 [32000, 896], P('tp', 'path'), may hold values from -0.375 to 0.375
- attn_outer: float32 [4, 896, 4096], P(None, 'path', 'tp'), may hold values from -0.0625 to 0.0625
- mlp_outer: float32 [4, 896, 7168], P(None, 'path', 'tp'), may hold values from -0.0625 to 0.0625
- gain_outer: float32 [4, 896, 2], P(None, 'path'), may hold values from -1.25 to 1.25
- table_outer: float32 [32000, 896], P('tp', 'path'), may hold values from -0.0625 to 0.0625
- attn_first: bfloat16 [8, 896, 4096], P('path', None, 'tp'), may hold values from -1.9073486e-06 to 1.9073486e-06
- mlp_first: bfloat16 [8, 896, 7168], P('path', None, 'tp'), may hold values from -1.9073486e-06 to 1.9073486e-06
- gain_first: bfloat16 [8, 896, 2], P('path'), may hold values from -9.536743e-06 to 9.536743e-06
- table_first: bfloat16 [32000, 896], P('tp', 'path'), may hold values from -1.1920929e-06 to 1.1920929e-06
- attn_second: bfloat16 [8, 896, 4096], P('path', None, 'tp'), may hold values from 5.222489e-13 to 2.0747848e-12
- mlp_second: bfloat16 [8, 896, 7168], P('path', None, 'tp'), may hold values from 5.222489e-13 to 2.0747848e-12
- gain_second: bfloat16 [8, 896, 2], P('path'), may hold values from 1.2846613e-11 to 5.2295945e-11
- table_second: bfloat16 [32000, 896], P('tp', 'path'), may hold values from 1.8474111e-13 to 7.31859e-13
Outputs:
- attn_new: float32 [4, 896, 4096], P(None, 'path', 'tp')
- mlp_new: float32 [4, 896, 7168], P(None, 'path', 'tp')
- gain_new: float32 [4, 896, 2], P(None, 'path')
- table_new: float32 [32000, 896], P('tp', 'path')
- attn_momentum: float32 [4, 896, 4096], P(None, 'path', 'tp')
- mlp_momentum: float32 [4, 896, 7168], P(None, 'path', 'tp')
- gain_momentum: float32 [4, 896, 2], P(None, 'path')
- table_momentum: float32 [32000, 896], P('tp', 'path')
- attn_first_new: float32 [8, 896, 4096], P('path', None, 'tp')
- mlp_first_new: float32 [8, 896, 7168], P('path', None, 'tp')
- gain_first_new: float32 [8, 896, 2], P('path')
- table_first_new: float32 [32000, 896], P('tp', 'path')
- attn_second_new: float32 [8, 896, 4096], P('path', None, 'tp')
- mlp_second_new: float32 [8, 896, 7168], P('path', None, 'tp')
- gain_second_new: float32 [8, 896, 2], P('path')
- table_second_new: float32 [32000, 896], P('tp', 'path')
- path_losses: float32 [8], P('path')
- path_norms: float32 [8], P('path')
- table_norm: float32 [], replicated
Inputs may be any that keep to these rules, and one draw needn't show every extreme that they name: `routes`: in each column every module of 0 to 3 is named by at least one path.
All inputs are finite; a program needn't handle non-finite values.
Results may differ from a plain program's by a relative error of at most 0.023.
Values may be sent and summed in bfloat16 or wider, within the bound.
No kernel may reach another device: no remote copies, remote signals or barrier semaphores. Data moves between devices by JAX's collectives and lax.ppermute only.
A program may use at most 384 MiB of HBM per device.

v0:
```python
import jax
import jax.numpy as jnp
from jax import lax
from jax.sharding import PartitionSpec as P

HEADS = 14
HEAD_DIM = 64
MODS = 4


norm_eps = 1e-05
adam_eps = 1e-08
beta_first = 0.9
beta_second = 0.95
rate_inner = 0.01
rate_gain = 1.0
rate_outer = 0.7
outer_mu = 0.9
decay_rate = 0.1
clip_limit = 0.01
step_count = 10


def normed(values):
    return values * lax.rsqrt(jnp.mean(values * values, -1, keepdims=True) + norm_eps)


def norm_back(values, upstream):
    inverse = lax.rsqrt(jnp.mean(values * values, -1, keepdims=True) + norm_eps)
    unit = values * inverse
    return inverse * (upstream - unit * jnp.mean(upstream * unit, -1, keepdims=True))


def rotate(values, positions, direction):
    halves = values.shape[-1] // 2
    freqs = 10000.0 ** (-jnp.arange(halves, dtype=jnp.float32) / halves)
    angles = positions.astype(jnp.float32)[:, None] * freqs
    cosine = jnp.cos(angles)[:, None, :]
    sine = direction * jnp.sin(angles)[:, None, :]
    first_half = values[..., :halves]
    second_half = values[..., halves:]
    return jnp.concatenate(
        [first_half * cosine - second_half * sine, second_half * cosine + first_half * sine], -1
    )


def segment_ids(doc_lengths, seq_len):
    bounds = jnp.cumsum(doc_lengths, -1)
    places = jnp.arange(seq_len, dtype=jnp.int32)
    return jnp.sum((places[None, :, None] >= bounds[:, None, :]).astype(jnp.int32), -1)


def block_scores(queries, keys, segments, index, block_len):
    blocks = queries.shape[1] // block_len
    row_index = index // blocks
    first_row = index % blocks * block_len
    query_rows = lax.dynamic_slice_in_dim(queries[row_index], first_row, block_len, 0)
    key_rows = keys[row_index]
    seg_row = segments[row_index]
    seg_query = lax.dynamic_slice_in_dim(seg_row, first_row, block_len, 0)
    scores = jnp.einsum(
        "qhe,khe->hqk", query_rows, key_rows, preferred_element_type=jnp.float32
    ) * queries.shape[-1] ** (-0.5)
    query_places = first_row + jnp.arange(block_len)
    key_places = jnp.arange(key_rows.shape[0])
    allowed = (seg_query[:, None] == seg_row[None, :]) & (
        key_places[None, :] <= query_places[:, None]
    )
    return (query_rows, jnp.where(allowed[None], scores, -1e30), row_index, first_row)


def attend_forward(queries, keys, values, segments, block_len):
    total_blocks = queries.shape[0] * (queries.shape[1] // block_len)

    def one_block(index):
        query_rows, scores, row_index, first_row = block_scores(
            queries, keys, segments, index, block_len
        )
        peak = jnp.max(scores, -1, keepdims=True)
        expo = jnp.exp(scores - peak)
        sums = jnp.sum(expo, -1, keepdims=True)
        probs = (expo / sums).astype(jnp.bfloat16)
        mixed = jnp.einsum(
            "hqk,khe->qhe", probs, values[row_index], preferred_element_type=jnp.float32
        )
        return (mixed, (peak + jnp.log(sums))[..., 0])

    mixed, log_sums = lax.map(one_block, jnp.arange(total_blocks))
    return (mixed.reshape(queries.shape), log_sums)


def attend_backward(queries, keys, values, segments, log_sums, grad_mixed, block_len):
    row_count, seq_len = queries.shape[:2]
    blocks = seq_len // block_len
    scale_factor = queries.shape[-1] ** (-0.5)

    def one_block(index):
        query_rows, scores, row_index, first_row = block_scores(
            queries, keys, segments, index, block_len
        )
        probs = jnp.exp(scores - log_sums[index][..., None])
        grad_rows = lax.dynamic_slice_in_dim(grad_mixed[row_index], first_row, block_len, 0)
        grad_probs = jnp.einsum(
            "qhe,khe->hqk", grad_rows, values[row_index], preferred_element_type=jnp.float32
        )
        inner = jnp.sum(probs * grad_probs, -1, keepdims=True)
        grad_scores = (probs * (grad_probs - inner)).astype(jnp.bfloat16)
        grad_query = (
            jnp.einsum(
                "hqk,khe->qhe", grad_scores, keys[row_index], preferred_element_type=jnp.float32
            )
            * scale_factor
        )
        grad_key = (
            jnp.einsum("hqk,qhe->khe", grad_scores, query_rows, preferred_element_type=jnp.float32)
            * scale_factor
        )
        grad_value = jnp.einsum(
            "hqk,qhe->khe",
            probs.astype(jnp.bfloat16),
            grad_rows,
            preferred_element_type=jnp.float32,
        )
        return (grad_query, grad_key, grad_value)

    grad_query, grad_key, grad_value = lax.map(one_block, jnp.arange(row_count * blocks))
    tail = keys.shape[1:]
    return (
        grad_query.reshape(queries.shape),
        grad_key.reshape((row_count, blocks) + tail).sum(1),
        grad_value.reshape((row_count, blocks) + tail).sum(1),
    )


def input_total(partial_grad):
    return lax.psum(partial_grad, "tp")


def branch_total(partial_branch):
    return lax.psum(partial_branch, "tp")


def layer_forward(hidden, attn_w, mlp_w, gain_w, segments, validity, block_len):
    row_count, seq_len, model_width = hidden.shape
    slot_cols = attn_w.shape[1] // 4
    places = jnp.arange(seq_len, dtype=jnp.int32)
    normed_in = (normed(hidden) * gain_w[:, 0].astype(jnp.float32)).astype(jnp.bfloat16)
    proj = jnp.einsum(
        "rsd,dc->rsc", normed_in, attn_w[:, : 3 * slot_cols], preferred_element_type=jnp.float32
    )
    proj = proj.reshape(row_count, seq_len, 3, validity.shape[0], -1)
    queries = rotate(proj[:, :, 0], places, 1.0).astype(jnp.bfloat16)
    keys = rotate(proj[:, :, 1], places, 1.0).astype(jnp.bfloat16)
    values = proj[:, :, 2].astype(jnp.bfloat16)
    mixed, log_sums = attend_forward(queries, keys, values, segments, block_len)
    mixed_low = (
        (mixed * validity[None, None, :, None])
        .astype(jnp.bfloat16)
        .reshape(row_count, seq_len, slot_cols)
    )
    branch = jnp.einsum(
        "rsc,dc->rsd", mixed_low, attn_w[:, 3 * slot_cols :], preferred_element_type=jnp.float32
    )
    hidden_mid = hidden + branch_total(branch)
    normed_mid = (normed(hidden_mid) * gain_w[:, 1].astype(jnp.float32)).astype(jnp.bfloat16)
    hidden_cols = mlp_w.shape[1] // 2
    upward = jnp.einsum(
        "rsd,df->rsf", normed_mid, mlp_w[:, :hidden_cols], preferred_element_type=jnp.float32
    )
    activ = jax.nn.gelu(upward, approximate=True).astype(jnp.bfloat16)
    branch_mlp = jnp.einsum(
        "rsf,df->rsd", activ, mlp_w[:, hidden_cols:], preferred_element_type=jnp.float32
    )
    hidden_out = hidden_mid + branch_total(branch_mlp)
    kept = (
        hidden,
        normed_in,
        queries,
        keys,
        values,
        log_sums,
        mixed_low,
        hidden_mid,
        normed_mid,
        upward,
        activ,
    )
    return (hidden_out, kept)


def layer_backward(grad_out, kept, attn_w, mlp_w, gain_w, segments, validity, block_len):
    (
        hidden,
        normed_in,
        queries,
        keys,
        values,
        log_sums,
        mixed_low,
        hidden_mid,
        normed_mid,
        upward,
        activ,
    ) = kept
    row_count, seq_len, model_width = hidden.shape
    slot_cols = attn_w.shape[1] // 4
    hidden_cols = mlp_w.shape[1] // 2
    places = jnp.arange(seq_len, dtype=jnp.int32)
    grad_branch = grad_out.astype(jnp.bfloat16)
    down_grad = jnp.einsum("rsd,rsf->df", grad_branch, activ, preferred_element_type=jnp.float32)
    grad_activ = jnp.einsum(
        "rsd,df->rsf", grad_branch, mlp_w[:, hidden_cols:], preferred_element_type=jnp.float32
    )
    unused, gelu_pull = jax.vjp(lambda inputs: jax.nn.gelu(inputs, approximate=True), upward)
    grad_up = gelu_pull(grad_activ)[0].astype(jnp.bfloat16)
    up_grad = jnp.einsum("rsd,rsf->df", normed_mid, grad_up, preferred_element_type=jnp.float32)
    grad_normed = input_total(
        jnp.einsum(
            "rsf,df->rsd", grad_up, mlp_w[:, :hidden_cols], preferred_element_type=jnp.float32
        )
    )
    gain_mlp = jnp.sum((grad_normed * normed(hidden_mid)).reshape(-1, model_width), 0)
    grad_mid = grad_out + norm_back(hidden_mid, grad_normed * gain_w[:, 1].astype(jnp.float32))
    grad_attn_out = grad_mid.astype(jnp.bfloat16)
    out_grad = jnp.einsum(
        "rsd,rsc->dc", grad_attn_out, mixed_low, preferred_element_type=jnp.float32
    )
    grad_mixed = jnp.einsum(
        "rsd,dc->rsc", grad_attn_out, attn_w[:, 3 * slot_cols :], preferred_element_type=jnp.float32
    )
    grad_mixed = (grad_mixed.reshape(queries.shape) * validity[None, None, :, None]).astype(
        jnp.bfloat16
    )
    grad_query, grad_key, grad_value = attend_backward(
        queries, keys, values, segments, log_sums, grad_mixed, block_len
    )
    grad_proj = jnp.stack(
        [rotate(grad_query, places, -1.0), rotate(grad_key, places, -1.0), grad_value], 2
    )
    grad_proj = grad_proj.reshape(row_count, seq_len, 3 * slot_cols).astype(jnp.bfloat16)
    proj_grad = jnp.einsum("rsd,rsc->dc", normed_in, grad_proj, preferred_element_type=jnp.float32)
    grad_normed_in = input_total(
        jnp.einsum(
            "rsc,dc->rsd", grad_proj, attn_w[:, : 3 * slot_cols], preferred_element_type=jnp.float32
        )
    )
    gain_attn = jnp.sum((grad_normed_in * normed(hidden)).reshape(-1, model_width), 0)
    grad_in = grad_mid + norm_back(hidden, grad_normed_in * gain_w[:, 0].astype(jnp.float32))
    attn_grad = jnp.concatenate([proj_grad, out_grad], 1)
    mlp_grad = jnp.concatenate([up_grad, down_grad], 1)
    return (grad_in, attn_grad, mlp_grad, jnp.stack([gain_attn, gain_mlp], -1))


def adam_moments(first, second, gradient):
    first_new = beta_first * first.astype(jnp.float32) + (1.0 - beta_first) * gradient
    second_new = (
        beta_second * second.astype(jnp.float32) + (1.0 - beta_second) * gradient * gradient
    )
    update = (
        first_new
        / (1.0 - beta_first**step_count)
        / (jnp.sqrt(second_new / (1.0 - beta_second**step_count)) + adam_eps)
    )
    return (first_new, second_new, update)


def outer_step(master, momentum, average, decay, rate):
    outer_grad = rate * (average + decay * master)
    moment_new = outer_mu * momentum + outer_grad
    return (master - rate_outer * (outer_grad + outer_mu * moment_new), moment_new)


def body(
    token_ids,
    targets,
    loss_positions,
    doc_lengths,
    live_tokens,
    routes,
    attn_master,
    mlp_master,
    gain_master,
    table_master,
    attn_outer,
    mlp_outer,
    gain_outer,
    table_outer,
    attn_first,
    mlp_first,
    gain_first,
    table_first,
    attn_second,
    mlp_second,
    gain_second,
    table_second,
):
    path_count = lax.axis_size("path")
    tp_count = lax.axis_size("tp")
    path_index = lax.axis_index("path")
    tp_index = lax.axis_index("tp")
    route_row = lax.dynamic_index_in_dim(routes, path_index, 0, keepdims=False)
    attn_pick = route_row[0]
    mlp_pick = route_row[1]
    model_width = attn_first.shape[1]
    rows_owned = attn_master.shape[1]
    attn_low = attn_master.astype(jnp.bfloat16)
    mlp_low = mlp_master.astype(jnp.bfloat16)
    gain_low = gain_master.astype(jnp.bfloat16)
    pieces = (
        lax.all_gather(attn_low, "path", axis=1, tiled=True),
        lax.all_gather(mlp_low, "path", axis=1, tiled=True),
        lax.all_gather(gain_low, "path", axis=1, tiled=True),
    )
    picked = (
        pieces[0][attn_pick],
        pieces[1][mlp_pick],
        jnp.stack([pieces[2][attn_pick, :, 0], pieces[2][mlp_pick, :, 1]], -1),
    )
    attn_w, mlp_w, gain_w = tuple((block_part for block_part in picked))
    table_w = lax.all_gather(table_master.astype(jnp.bfloat16), "path", axis=1, tiled=True)
    counts = lax.all_gather(
        jnp.sum(live_tokens).astype(jnp.float32)[None], "path", axis=0, tiled=True
    )
    row_count, seq_len = token_ids.shape
    block_len = min(512, seq_len)
    vocab_part = table_w.shape[0]
    offset = tp_index * vocab_part
    segments = segment_ids(doc_lengths, seq_len)
    slot_dev = attn_w.shape[1] // 4
    head_size = HEAD_DIM
    slots_here = slot_dev // head_size
    missing = tp_count * slots_here - HEADS
    limit = slots_here - (tp_index >= tp_count - missing).astype(jnp.int32)
    validity = (jnp.arange(slots_here) < limit).astype(jnp.float32)
    local_ids = token_ids - offset
    inside = (local_ids >= 0) & (local_ids < vocab_part)
    clipped_ids = jnp.clip(local_ids, 0, vocab_part - 1)
    looked = jnp.where(inside[..., None], table_w[clipped_ids], jnp.zeros((), jnp.bfloat16))
    hidden = lax.psum(looked, "tp").astype(jnp.float32)
    hidden_out, kept = layer_forward(hidden, attn_w, mlp_w, gain_w, segments, validity, block_len)
    final_rows = jnp.take_along_axis(hidden_out, loss_positions[..., None], 1).reshape(
        -1, model_width
    )
    head_in = normed(final_rows).astype(jnp.bfloat16)
    logits = jnp.einsum("nd,vd->nv", head_in, table_w, preferred_element_type=jnp.float32)
    top_logit = lax.pmax(jnp.max(logits, -1), "tp")
    expo = jnp.exp(logits - top_logit[:, None])
    local_targets = targets.reshape(-1) - offset
    hit = (local_targets >= 0) & (local_targets < vocab_part)
    clipped_targets = jnp.clip(local_targets, 0, vocab_part - 1)
    picked = jnp.where(hit, jnp.take_along_axis(logits, clipped_targets[:, None], 1)[:, 0], 0.0)
    totals, target_logit = lax.psum((jnp.sum(expo, -1), picked), "tp")
    log_total = top_logit + jnp.log(totals)
    position_count = logits.shape[0]
    path_loss = jnp.mean(log_total - target_logit)
    onehot = (jnp.arange(vocab_part)[None, :] == clipped_targets[:, None]) & hit[:, None]
    grad_logits = ((expo / totals[:, None] - onehot.astype(jnp.float32)) / position_count).astype(
        jnp.bfloat16
    )
    table_grad = jnp.einsum("nv,nd->vd", grad_logits, head_in, preferred_element_type=jnp.float32)
    grad_head = input_total(
        jnp.einsum("nv,vd->nd", grad_logits, table_w, preferred_element_type=jnp.float32)
    )
    grad_final = norm_back(final_rows, grad_head).reshape(row_count, -1, model_width)
    row_numbers = jnp.broadcast_to(jnp.arange(row_count)[:, None], loss_positions.shape)
    grad_out = (
        jnp.zeros(hidden_out.shape, jnp.float32).at[row_numbers, loss_positions].add(grad_final)
    )
    grad_in, attn_grad, mlp_grad, gain_grad = layer_backward(
        grad_out, kept, attn_w, mlp_w, gain_w, segments, validity, block_len
    )
    table_grad = table_grad.at[clipped_ids.reshape(-1)].add(
        jnp.where(inside.reshape(-1, 1), grad_in.reshape(-1, model_width), 0.0)
    )
    local_squares = (
        jnp.sum(attn_grad * attn_grad)
        + jnp.sum(mlp_grad * mlp_grad)
        + jnp.sum(gain_grad * gain_grad) / tp_count
    )
    path_norm = jnp.sqrt(lax.psum(local_squares, "tp"))
    factor = jnp.minimum(1.0, clip_limit / (path_norm + 1e-06))
    a_first_new, a_second_new, a_update = adam_moments(
        attn_first[0], attn_second[0], attn_grad * factor
    )
    m_first_new, m_second_new, m_update = adam_moments(
        mlp_first[0], mlp_second[0], mlp_grad * factor
    )
    g_first_new, g_second_new, g_update = adam_moments(
        gain_first[0], gain_second[0], gain_grad * factor
    )
    table_part = lax.psum_scatter(
        table_grad.astype(jnp.bfloat16), "path", scatter_dimension=1, tiled=True
    ).astype(jnp.float32)
    table_norm = jnp.sqrt(lax.psum(jnp.sum(table_part * table_part), ("path", "tp")))
    table_clip = table_part * jnp.minimum(1.0, clip_limit / (table_norm + 1e-06))
    t_first_new, t_second_new, t_update = adam_moments(table_first, table_second, table_clip)
    weight = lax.dynamic_index_in_dim(counts, path_index, 0, keepdims=False)
    scaled_attn = weight * a_update
    scaled_mlp = weight * m_update
    scaled_gain = weight * g_update
    module_ids = jnp.arange(MODS)
    pick_attn = (routes[:, 0][None, :] == module_ids[:, None]).astype(jnp.float32)
    pick_mlp = (routes[:, 1][None, :] == module_ids[:, None]).astype(jnp.float32)
    outgoing = (
        scaled_attn.reshape(path_count, rows_owned, -1),
        scaled_mlp.reshape(path_count, rows_owned, -1),
        scaled_gain.reshape(path_count, rows_owned, 2),
    )
    incoming = (
        lax.all_to_all(
            outgoing[0].astype(jnp.bfloat16), "path", split_axis=0, concat_axis=0, tiled=True
        ).astype(jnp.float32),
        lax.all_to_all(
            outgoing[1].astype(jnp.bfloat16), "path", split_axis=0, concat_axis=0, tiled=True
        ).astype(jnp.float32),
        lax.all_to_all(
            outgoing[2].astype(jnp.bfloat16), "path", split_axis=0, concat_axis=0, tiled=True
        ).astype(jnp.float32),
    )
    highest = lax.Precision.HIGHEST
    attn_total = jnp.einsum("mq,qrc->mrc", pick_attn, incoming[0], precision=highest)
    mlp_total = jnp.einsum("mq,qrc->mrc", pick_mlp, incoming[1], precision=highest)
    gain_total = jnp.stack(
        [
            jnp.einsum("mq,qr->mr", pick_attn, incoming[2][..., 0], precision=highest),
            jnp.einsum("mq,qr->mr", pick_mlp, incoming[2][..., 1], precision=highest),
        ],
        -1,
    )
    den_attn = jnp.sum(pick_attn * counts[None, :], 1)
    den_mlp = jnp.sum(pick_mlp * counts[None, :], 1)
    attn_new, attn_momentum = outer_step(
        attn_master, attn_outer, attn_total / den_attn[:, None, None], decay_rate, rate_inner
    )
    mlp_new, mlp_momentum = outer_step(
        mlp_master, mlp_outer, mlp_total / den_mlp[:, None, None], decay_rate, rate_inner
    )
    gain_new, gain_momentum = outer_step(
        gain_master,
        gain_outer,
        gain_total / jnp.stack([den_attn, den_mlp], -1)[:, None, :],
        0.0,
        rate_gain,
    )
    table_new, table_momentum = outer_step(
        table_master, table_outer, t_update, decay_rate, rate_inner
    )
    return (
        attn_new,
        mlp_new,
        gain_new,
        table_new,
        attn_momentum,
        mlp_momentum,
        gain_momentum,
        table_momentum,
        a_first_new[None],
        m_first_new[None],
        g_first_new[None],
        t_first_new,
        a_second_new[None],
        m_second_new[None],
        g_second_new[None],
        t_second_new,
        path_loss[None],
        path_norm[None],
        table_norm,
    )


def solution(mesh):
    in_specs = (
        P("path", None),
        P("path", None),
        P("path", None),
        P("path", None),
        P("path"),
        P(),
        P(None, "path", "tp"),
        P(None, "path", "tp"),
        P(None, "path", None),
        P("tp", "path"),
        P(None, "path", "tp"),
        P(None, "path", "tp"),
        P(None, "path", None),
        P("tp", "path"),
        P("path", None, "tp"),
        P("path", None, "tp"),
        P("path", None, None),
        P("tp", "path"),
        P("path", None, "tp"),
        P("path", None, "tp"),
        P("path", None, None),
        P("tp", "path"),
    )
    out_specs = (
        P(None, "path", "tp"),
        P(None, "path", "tp"),
        P(None, "path", None),
        P("tp", "path"),
        P(None, "path", "tp"),
        P(None, "path", "tp"),
        P(None, "path", None),
        P("tp", "path"),
        P("path", None, "tp"),
        P("path", None, "tp"),
        P("path", None, None),
        P("tp", "path"),
        P("path", None, "tp"),
        P("path", None, "tp"),
        P("path", None, None),
        P("tp", "path"),
        P("path"),
        P("path"),
        P(),
    )
    return jax.shard_map(body, mesh=mesh, in_specs=in_specs, out_specs=out_specs, check_vma=False)
```

profile of v0, /device:TPU:0, one launch (start us, length us, event | category | flops | bytes accessed | tf_op | source)
XLA Modules:
  0.0 1563.3 jit_solution(10924259591897857003)
XLA Ops:
  12.1 200.8 %all-gather.4.cloned.1.call-done = bf16[8000,896]{0,1:T(8,128)(2,1)} async-done(((bf16[8000,112]{0,1:T(8,128)(2,1)}), bf16[8000,896]{0,1:T(8,128)(2,1)}) %all-gather.4.cloned.1.call-update) | async-done | bytes 14336016 | tf_op jit(solution)/shard_map/all_gather | solution.py:320
  212.9 19.4 %copy.218 = bf16[8000,896]{1,0:T(8,128)(2,1)} copy(bf16[8000,896]{0,1:T(8,128)(2,1)} %all-gather.4.cloned.1.call-done) | data formatting | bytes 28672000 | tf_op jit(solution)/shard_map/all_gather | solution.py:320
  232.3 11.6 gather_fusion
  253.9 32.8 %all_gather.17 = bf16[4,896,2]{0,2,1:T(2,128)(2,1)S(1)} all-gather(bf16[4,112,2]{0,2,1:T(2,128)(2,1)S(1)} %copy.220), channel_id=1, replica_groups=mesh['path'=8,'tp'=4] {'path'}, dimensions={1}, use_global_device_ids=true | all-gather | bytes 16128 | tf_op jit(solution)/shard_map/all_gather | solution.py:312
  286.7 6.1 convert_reduce_fusion
  294.2 37.3 %all-gather.6.cloned.1.call-done = bf16[4,896,1024]{2,1,0:T(8,128)(2,1)} async-done(((bf16[4,112,1024]{2,1,0:T(8,128)(2,1)}), bf16[4,896,1024]{2,1,0:T(8,128)(2,1)}) %all-gather.6.cloned.1.call-update) | async-done | bytes 7340048 | tf_op jit(solution)/shard_map/all_gather | solution.py:310
  335.5 44.8 %all-reduce.10.cloned.1.call-done = bf16[1,1024,896]{2,1,0:T(8,128)(2,1)} async-done(((bf16[1,1024,896]{2,1,0:T(8,128)(2,1)}), bf16[1,1024,896]{2,1,0:T(8,128)(2,1)}) %all-reduce.10.cloned.1.call-update) | async-done | bytes 1835024 | tf_op jit(solution)/shard_map/psum | solution.py:339
  387.2 19.7 %while.30 = (s32[]{:T(128)}, f32[2,512,4,64]{1,3,2,0:T(8,128)S(1)}, f32[2,4,512]{2,1,0:T(4,128)S(1)}, s32[2]{0:T(128)S(1)}, s32[1,1024]{1,0:T(1,128)S(1)}, /*ind...) while((s32[]{:T(128)}, f32[2,512,4,64]{1,3,2,0:T(8,128)S(1)}, ...), condition=%wide.region_7.8_spmd, body=%wide.region_4.7_spmd.sunk | while | flops 563608064 | bytes 29178168 | solution.py:88
  412.1 150.6 %all-gather.8.cloned.1.call-done = bf16[4,896,1792]{2,1,0:T(8,128)(2,1)} async-done(((bf16[4,112,1792]{2,1,0:T(8,128)(2,1)}), bf16[4,896,1792]{2,1,0:T(8,128)(2,1)}) %all-gather.8.cloned.1.call-update) | async-done | bytes 12845072 | tf_op jit(solution)/shard_map/all_gather | solution.py:311
  566.5 74.2 %all-reduce.12.cloned.1.call-done = f32[1,1024,896]{2,1,0:T(8,128)} async-done(((f32[1,1024,896]{2,1,0:T(8,128)}), f32[1,1024,896]{2,1,0:T(8,128)}) %all-reduce.12.cloned.1.call-update) | async-done | bytes 3670032 | tf_op jit(solution)/shard_map/psum | solution.py:140
  653.9 76.1 %all-reduce.14.cloned.1.call-done = f32[1,1024,896]{2,1,0:T(8,128)} async-done(((f32[1,1024,896]{2,1,0:T(8,128)}), f32[1,1024,896]{2,1,0:T(8,128)}) %all-reduce.14.cloned.1.call-update) | async-done | bytes 3670032 | tf_op jit(solution)/shard_map/psum | solution.py:140
  738.6 12.6 fusion.192
  751.2 6.0 pmax.7
  760.4 5.7 psum.73
  766.1 11.8 fusion.187
  777.9 33.9 %all-reduce.16.cloned.1.call-done = f32[128,896]{1,0:T(8,128)} async-done(((f32[128,896]{1,0:T(8,128)}), f32[128,896]{1,0:T(8,128)}) %all-reduce.16.cloned.1.call-update) | async-done | bytes 458768 | tf_op jit(solution)/shard_map/psum | solution.py:136
  817.4 7.7 fusion.71
  832.2 75.3 %all-reduce.18.cloned.1.call-done = f32[1,1024,896]{2,1,0:T(8,128)} async-done(((f32[1,1024,896]{2,1,0:T(8,128)}), f32[1,1024,896]{2,1,0:T(8,128)}) %all-reduce.18.cloned.1.call-update) | async-done | bytes 3670032 | tf_op jit(solution)/shard_map/psum | solution.py:136
  918.3 76.7 %while.31 = (s32[]{:T(128)}, f32[2,512,4,64]{1,0,3,2:T(2,128)}, f32[2,1024,4,64]{1,3,2,0:T(8,128)}, f32[2,1024,4,64]{1,3,2,0:T(8,128)}, s32[2]{0:T(128)S(1)}, /*...) while((s32[]{:T(128)}, f32[2,512,4,64]{1,0,3,2:T(2,128)}, ...), condition=%wide.region_23.24_spmd, body=%wide.region_21.23_spmd.sunk | while | flops 1375599104 | bytes 101785040 | solution.py:126
  927.4 5.8 multiply_reduce_fusion.7
  939.4 10.4 dynamic_update_slice.46
  949.8 6.8 fusion.239
  965.6 5.8 multiply_reduce_fusion.7
  977.7 10.4 dynamic_update_slice.46
  988.1 6.8 fusion.239
  1007.0 16.2 %fusion.180 = f32[8000,896]{1,0:T(8,128)} fusion(f32[128,896]{1,0:T(8,128)S(1)} %gather_fusion.1, f32[128]{0:T(128)S(1)} %add_rsqrt_fusion.2, pred[128]{0:T(512)(128)(4,1)S(1)} %compare_and_fusion, f32[128,8000]{0,1:T(8,128)} %get-tuple-element.482, s32[128]{0:T(128)S(1)} %clamp_bitcast_fusion, f32[128]{0:T(128)S(1)} %psum.73, f32[128]{0:T(128)S(1)} %pmax.7, ...), kind=kOutput, calls=%fused_computation.314 | convolution fusion | flops 1843544064 | bytes 33229056 | tf_op jit(solution)/shard_map/nv,nd->vd/dot_general | solution.py:360
  1023.2 60.3 %all-reduce.20.cloned.1.call-done = f32[1,1024,896]{2,1,0:T(8,128)} async-done(((f32[1,1024,896]{2,1,0:T(8,128)}), f32[1,1024,896]{2,1,0:T(8,128)}) %all-reduce.20.cloned.1.call-update) | async-done | bytes 3670032 | tf_op jit(solution)/shard_map/psum | solution.py:136
  1086.7 30.1 %scatter_custom_fusion.1 = f32[8000,896]{1,0:T(8,128)} fusion(f32[8000,896]{1,0:T(8,128)} %fusion.180, s32[1024]{0:T(1024)S(1)} %bitcast.332, f32[1,1024,896]{2,1,0:T(8,128)} %copy-done, bf16[1,1024,896]{2,1,0:T(8,128)(2,1)S(1)} %copy-done.4, f32[1,1024,896]{2,1,0:T(8,128)} %all-reduce.20.cloned.1.call-done, f32[]{:T(128)} %constant.301.clone.1, ...), kind=kCustom, calls=%fused_computation.120 | custom fusion | flops 8257536 | bytes 37860864 | tf_op jit(solution)/shard_map/scatter-add | solution.py:372
  1116.8 16.0 %convert_element_type.324 = bf16[8000,896]{1,0:T(8,128)(2,1)} convert(f32[8000,896]{1,0:T(8,128)} %scatter_custom_fusion.1) | non-fusion elementwise | flops 7168000 | bytes 43008000 | tf_op jit(solution)/shard_map/convert_element_type | solution.py:392
  1132.8 19.4 %copy.256 = bf16[8000,896]{0,1:T(8,128)(2,1)} copy(bf16[8000,896]{1,0:T(8,128)(2,1)} %convert_element_type.324) | data formatting | bytes 28672000
  1154.3 22.2 %all-reduce.1 = f32[8]{0:T(128)S(1)} all-reduce(f32[8]{0:T(128)S(1)} %convert_dynamic-update-slice_fusion), channel_id=1, replica_groups=mesh['path'=8,'tp'=4] {'path'}, use_global_device_ids=true, to_apply=%add.1 | all-reduce | flops 8 | bytes 64
  1202.2 6.5 all-reduce.2
  1215.4 5.7 fusion.89
  1225.1 6.1 all-to-all-start
  1231.2 10.3 fusion.53
  1241.5 8.1 fusion.55
  1249.6 67.1 %all-to-all-done = bf16[8,112,1024]{2,1,0:T(8,128)(2,1)} async-done(((bf16[8,112,1024]{2,1,0:T(8,128)(2,1)}), bf16[8,112,1024]{2,1,0:T(8,128)(2,1)}, u32[]{:S(2)}, u32[]{:S(2)}) %all-to-all-start) | async-done | bytes 1835040 | tf_op jit(solution)/shard_map/all_to_all | solution.py:410
  1321.2 5.4 copy.244
  1343.1 6.4 fusion.107
  1354.1 38.2 %all-to-all-done.1 = bf16[8,112,1792]{2,1,0:T(8,128)(2,1)} async-done(((bf16[8,112,1792]{2,1,0:T(8,128)(2,1)}), bf16[8,112,1792]{2,1,0:T(8,128)(2,1)}, u32[]{:S(2)}, u32[]{:S(2)}) %all-to-all-start.1) | async-done | bytes 3211296 | tf_op jit(solution)/shard_map/all_to_all | solution.py:413
  1392.3 8.7 fusion.94
  1403.3 60.8 %reduce-scatter.4.cloned.1.call-done = bf16[112,8000]{1,0:T(8,128)(2,1)} async-done(((bf16[896,8000]{1,0:T(8,128)(2,1)}), bf16[112,8000]{1,0:T(8,128)(2,1)}) %reduce-scatter.4.cloned.1.call-update) | async-done | bytes 1792016
  1473.3 39.5 %psum.78 = f32[]{:T(128)} all-reduce(f32[]{:T(128)} %fusion.62), channel_id=1, replica_groups=mesh['path'=8,'tp'=4] {'path','tp'}, use_global_device_ids=true, to_apply=%region_39.40 | all-reduce | flops 1 | bytes 8 | tf_op jit(solution)/shard_map/psum | solution.py:394
  1513.6 9.0 multiply_add_fusion.1
  1522.6 5.4 copy.253
  1528.0 8.5 multiply_subtract_fusion
  1536.5 5.4 copy.254
  1547.4 5.4 copy.252
  (331 shorter events, 211.6 us)
Async XLA Ops:
  7.2 205.7 %all-gather.4.cloned.1.call-start = ((), (), s32[]{:S(2)}) async-start(), calls=%async_computation.4 | async-start | bytes 16257024 | tf_op jit(solution)/shard_map/all_gather | solution.py:320
  10.8 320.6 %all-gather.6.cloned.1.call-start = ((), (), s32[]{:S(2)}) async-start(), calls=%async_computation.6 | async-start | bytes 8257536 | tf_op jit(solution)/shard_map/all_gather | solution.py:310
  12.0 368.3 %all-reduce.10.cloned.1.call-start = ((), (), s32[]{:S(2)}) async-start(), calls=%async_computation.5 | async-start | bytes 3670016 | tf_op jit(solution)/shard_map/psum | solution.py:339
  12.1 231.9 %copy-start.47 = (pred[1024]{0:T(1024)(128)(4,1)}, pred[1024]{0:T(1024)(128)(4,1)S(1)}, u32[]{:S(2)}) copy-start(pred[1024]{0:T(1024)(128)(4,1)S(1)} %and_reduce_fusion) | copy-start | bytes 3076
  245.5 6.6 copy-start.45
  245.5 6.8 copy-start.58
  245.5 317.1 %all-gather.8.cloned.1.call-start = ((), (), s32[]{:S(2)}) async-start(), calls=%async_computation.8 | async-start | bytes 14450688 | tf_op jit(solution)/shard_map/all_gather | solution.py:311
  248.8 391.8 %all-reduce.12.cloned.1.call-start = ((), (), s32[]{:S(2)}) async-start(), calls=%async_computation.7 | async-start | bytes 7340032 | tf_op jit(solution)/shard_map/psum | solution.py:140
  252.5 79.0 %copy-start.42 = (f32[4]{0:T(128)}, f32[4]{0:T(128)S(1)}, u32[]{:S(2)}) copy-start(f32[4]{0:T(128)S(1)} %compare_convert_fusion) | copy-start | bytes 52
  292.9 89.4 %copy-start.34 = (f32[896]{0:T(1024)}, f32[896]{0:T(1024)S(1)}, u32[]{:S(2)}) copy-start(f32[896]{0:T(1024)S(1)} %get-tuple-element.386) | copy-start | bytes 10756
  292.9 619.5 %copy-start.38 = (f32[896]{0:T(1024)}, f32[896]{0:T(1024)S(1)}, u32[]{:S(2)}) copy-start(f32[896]{0:T(1024)S(1)} %get-tuple-element.385) | copy-start | bytes 10756
  294.2 91.8 %copy-start.28 = (f32[1024,32]{0,1:T(8,128)}, f32[1024,32]{0,1:T(8,128)S(1)}, u32[]{:S(2)}) copy-start(f32[1024,32]{0,1:T(8,128)S(1)} %get-tuple-element.472) | copy-start | bytes 393220
  411.6 318.4 %all-reduce.14.cloned.1.call-start = ((), (), s32[]{:S(2)}) async-start(), calls=%async_computation.9 | async-start | bytes 7340032 | tf_op jit(solution)/shard_map/psum | solution.py:140
  644.0 268.4 %copy-start.40 = (f32[1024]{0:T(1024)}, f32[1024]{0:T(1024)S(1)}, u32[]{:S(2)}) copy-start(f32[1024]{0:T(1024)S(1)} %add_rsqrt_fusion) | copy-start | bytes 12292
  652.7 159.1 %all-reduce.16.cloned.1.call-start = ((), (), s32[]{:S(2)}) async-start(), calls=%async_computation.10 | async-start | bytes 917504 | tf_op jit(solution)/shard_map/psum | solution.py:136
  653.9 81.4 %copy-start.56 = (s32[1,128]{1,0:T(1,128)}, s32[1,128]{1,0:T(1,128)S(1)}, u32[]{:S(2)}) copy-start(s32[1,128]{1,0:T(1,128)S(1)} %get-tuple-element.433) | copy-start | bytes 1540
  777.9 129.7 %all-reduce.18.cloned.1.call-start = ((), (), s32[]{:S(2)}) async-start(), calls=%async_computation.11 | async-start | bytes 7340032 | tf_op jit(solution)/shard_map/psum | solution.py:136
  817.4 8.9 copy-start.21
  830.4 253.2 %all-reduce.20.cloned.1.call-start = ((), (), s32[]{:S(2)}) async-start(), calls=%async_computation.12 | async-start | bytes 7340032 | tf_op jit(solution)/shard_map/psum | solution.py:136
  918.3 9.0 copy-start.15
  927.4 5.9 slice-start.1
  949.8 6.8 copy-start.16
  956.6 9.0 copy-start.15
  988.1 6.8 copy-start.16
  1006.3 457.8 %reduce-scatter.4.cloned.1.call-start = ((), (), s32[]{:S(2)}) async-start(), calls=%async_computation.13 | async-start | bytes 16257024
  1007.0 76.6 %copy-start.4 = (bf16[1,1024,896]{2,1,0:T(8,128)(2,1)S(1)}, bf16[1,1024,896]{2,1,0:T(8,128)(2,1)}, u32[]{:S(2)}) copy-start(bf16[1,1024,896]{2,1,0:T(8,128)(2,1)} %all-reduce.10.cloned.1.call-done) | copy-start | bytes 5505028
  1007.0 76.6 %copy-start.35 = (f32[896]{0:T(1024)S(1)}, f32[896]{0:T(1024)}, u32[]{:S(2)}) copy-start(f32[896]{0:T(1024)} %copy-done.34) | copy-start | bytes 10756
  1007.0 76.6 %copy-start.37 = (f32[1024]{0:T(1024)S(1)}, f32[1024]{0:T(1024)}, u32[]{:S(2)}) copy-start(f32[1024]{0:T(1024)} %copy-done.36) | copy-start | bytes 12292
  1023.2 63.4 %copy-start.48 = (pred[1024]{0:T(1024)(128)(4,1)S(1)}, pred[1024]{0:T(1024)(128)(4,1)}, u32[]{:S(2)}) copy-start(pred[1024]{0:T(1024)(128)(4,1)} %copy-done.47) | copy-start | bytes 3076
  1152.2 25.0 %copy-start.54 = (s32[128,1,1]{0,2,1:T(1,128)S(1)}, s32[128,1,1]{0,2,1:T(1,128)}, u32[]{:S(2)}) copy-start(s32[128,1,1]{0,2,1:T(1,128)} %get-tuple-element.432) | copy-start | bytes 1540
  1152.2 25.0 %copy-start.19 = (f32[2,512,4,64]{1,3,2,0:T(8,128)S(1)}, f32[2,512,4,64]{1,3,2,0:T(8,128)}, u32[]{:S(2)}) copy-start(f32[2,512,4,64]{1,3,2,0:T(8,128)} %copy-done.18) | copy-start | bytes 3145732
  1152.2 25.0 %copy-start.44 = (f32[4]{0:T(128)S(1)}, f32[4]{0:T(128)}, u32[]{:S(2)}) copy-start(f32[4]{0:T(128)} %copy-done.42) | copy-start | bytes 52
  1152.2 30.9 %copy-start.57 = (s32[1,128]{1,0:T(1,128)S(1)}, s32[1,128]{1,0:T(1,128)}, u32[]{:S(2)}) copy-start(s32[1,128]{1,0:T(1,128)} %copy-done.56) | copy-start | bytes 1540
  1152.2 30.9 %copy-start.39 = (f32[896]{0:T(1024)S(1)}, f32[896]{0:T(1024)}, u32[]{:S(2)}) copy-start(f32[896]{0:T(1024)} %copy-done.38) | copy-start | bytes 10756
  1152.2 30.9 %copy-start.41 = (f32[1024]{0:T(1024)S(1)}, f32[1024]{0:T(1024)}, u32[]{:S(2)}) copy-start(f32[1024]{0:T(1024)} %copy-done.40) | copy-start | bytes 12292
  1197.9 11.6 copy-start.52
  1197.9 11.6 copy-start.53
  1197.9 17.4 %copy-start.23 = (bf16[1,896,1024]{2,1,0:T(8,128)(2,1)S(1)}, bf16[1,896,1024]{2,1,0:T(8,128)(2,1)}, u32[]{:S(2)}) copy-start(bf16[1,896,1024]{2,1,0:T(8,128)(2,1)} %param.44) | copy-start | bytes 5505028
  1211.6 13.5 all-to-all-start.2
  1225.1 6.1 copy-start.6
  1225.1 91.5 %all-to-all-start = ((bf16[8,112,1024]{2,1,0:T(8,128)(2,1)}), bf16[8,112,1024]{2,1,0:T(8,128)(2,1)}, u32[]{:S(2)}, u32[]{:S(2)}) async-start(bf16[8,112,1024]{2,1,0:T(8,128)(2,1)} %fusion.91), calls=%async_computation | async-start | bytes 3670016 | tf_op jit(solution)/shard_map/all_to_all | solution.py:410
  1231.2 10.3 copy-start.8
  1316.6 75.7 %all-to-all-start.1 = ((bf16[8,112,1792]{2,1,0:T(8,128)(2,1)}), bf16[8,112,1792]{2,1,0:T(8,128)(2,1)}, u32[]{:S(2)}, u32[]{:S(2)}) async-start(bf16[8,112,1792]{2,1,0:T(8,128)(2,1)} %fusion.55), calls=%async_computation.1 | async-start | bytes 6422528 | tf_op jit(solution)/shard_map/all_to_all | solution.py:413
  1332.1 8.0 copy-start.50
  1332.1 9.7 copy-start.46
  1332.1 9.7 copy-start.51
  1332.1 11.0 copy-start.25
  1349.5 42.8 %copy-start.22 = (f32[4,112,1792]{2,1,0:T(8,128)S(1)}, f32[4,112,1792]{2,1,0:T(8,128)}, u32[]{:S(2)}) copy-start(f32[4,112,1792]{2,1,0:T(8,128)} %param.33) | copy-start | bytes 9633796
  (35 other events, 110.7 us)
Sparse Core Ops, SparseCore 0:
  11.0 201.9 all-gather.3
  215.7 115.7 all-gather.5
  334.4 45.8 all-reduce.9
  382.9 179.6 all-gather.7
  565.5 75.1 all-reduce.11
  652.8 77.0 all-reduce.13
  778.0 33.8 all-reduce.15
  830.5 76.9 all-reduce.17
  1006.4 77.0 all-reduce.19
  1152.3 311.7 reduce-scatter.3
where the time goes:
time: 1580 us; the launch traced here: 1560 us
  waiting for transfers between devices  919 us (58%)
  local copies, waits for them, and re-layouts  167 us (11%)
  other arithmetic  165 us (10%)
  matrix products  145 us (9%)
  blocking collectives  113 us (7%)
  between operations  27.6 us (2%)
    all_gather x1, waiting for transfers between devices, body(): lax.all_gather(table_master.astype(jnp.bfloat16), 'path', axis=1, tiled=T...  201 us
    psum x3, waiting for transfers between devices, input_total(): return lax.psum(partial_grad, 'tp')  170 us
    all_gather x1, waiting for transfers between devices, body(): lax.all_gather(mlp_low, 'path', axis=1, tiled=True)  151 us
    psum x2, waiting for transfers between devices, branch_total(): return lax.psum(partial_branch, 'tp')  150 us
    unnamed x146, local copies, waits for them, and re-layouts  89 us
    all_to_all x1, waiting for transfers between devices, body(): lax.all_to_all(outgoing[0].astype(jnp.bfloat16), 'path', split_axis=0, co...  67.1 us
    unnamed x11, waiting for transfers between devices  61 us
    psum x1, waiting for transfers between devices, body(): hidden = lax.psum(looked, 'tp').astype(jnp.float32)  44.8 us
  transfers between devices with their start and end apart: 13, of which 12 were waited for; matrix products, arithmetic and copies ran while one was open for 12% of the time, Pallas kernels for 0%

commit v1 on v0

v1 whole, which is shorter than its diff:
```python
import jax
import jax.numpy as jnp
from jax import lax
from jax.experimental import pallas as pl
from jax.experimental.pallas import tpu as pltpu
from jax.sharding import PartitionSpec as P

HEADS = 14
HEAD_DIM = 64
MODS = 4
LANES = 128

bf16 = jnp.bfloat16
f32 = jnp.float32

norm_eps = 1e-05
adam_eps = 1e-08
beta_first = 0.9
beta_second = 0.95
rate_inner = 0.01
rate_gain = 1.0
rate_outer = 0.7
outer_mu = 0.9
decay_rate = 0.1
clip_limit = 0.01
step_count = 10


def normed(values):
    return values * lax.rsqrt(jnp.mean(values * values, -1, keepdims=True) + norm_eps)


def norm_back(values, upstream):
    inverse = lax.rsqrt(jnp.mean(values * values, -1, keepdims=True) + norm_eps)
    unit = values * inverse
    return inverse * (upstream - unit * jnp.mean(upstream * unit, -1, keepdims=True))


def dot(left, right, dims):
    return lax.dot_general(left, right, (dims, ((), ())), preferred_element_type=f32)


def angle_tables(positions, copies):
    halves = HEAD_DIM // 2
    freqs = 10000.0 ** (-jnp.arange(halves, dtype=f32) / halves)
    angles = positions.astype(f32)[:, None] * freqs
    cosine = jnp.cos(angles)
    sine = jnp.sin(angles)
    return (
        jnp.tile(jnp.concatenate([cosine, cosine], -1), (1, copies)),
        jnp.tile(jnp.concatenate([-sine, sine], -1), (1, copies)),
    )


def swapped(values):
    halves = HEAD_DIM // 2
    rows, columns = values.shape
    split = values.reshape(rows, columns // HEAD_DIM, 2, halves)
    return jnp.concatenate([split[:, :, 1:], split[:, :, :1]], 2).reshape(rows, columns)


def rotate(values, tables):
    return values * tables[0] + swapped(values) * tables[1]


def rotate_back(values, tables):
    return values * tables[0] - swapped(values) * tables[1]


def swap(value, axis, step):
    count = lax.axis_size(axis)
    return lax.ppermute(value, axis, [(i, i ^ step) for i in range(count)])


def halves_of(value, bit):
    mine = lax.dynamic_index_in_dim(value, bit, 1, keepdims=False)
    other = lax.dynamic_index_in_dim(value, 1 - bit, 1, keepdims=False)
    return mine, other


def tp_scatter(parts):
    index = lax.axis_index("tp")
    tail = parts.shape[1:]
    mine, other = halves_of(parts.reshape((2, 2) + tail), index % 2)
    got = swap(other.astype(bf16), "tp", 1)
    both = (mine + got.astype(f32))[None]
    mine, other = halves_of(both, index // 2)
    got = swap(other.astype(bf16), "tp", 2)
    return (mine + got.astype(f32))[0]


def joined(mine, other, bit, axis):
    low = jnp.where(bit == 0, mine, other)
    high = jnp.where(bit == 0, other, mine)
    return jnp.stack([low, high], axis)


def tp_gather(part):
    index = lax.axis_index("tp")
    pair = joined(part, swap(part, "tp", 2), index // 2, 0)
    whole = joined(pair, swap(pair, "tp", 1), index % 2, 1)
    return whole.reshape((4,) + part.shape)


def tp_total(partial):
    rows = partial.shape[0]
    part = tp_scatter(partial.reshape((4, rows // 4) + partial.shape[1:]))
    return tp_gather(part.astype(bf16)).reshape(partial.shape).astype(f32)


def butterfly(value, axis):
    step = 1
    while step < lax.axis_size(axis):
        value = value + swap(value, axis, step)
        step *= 2
    return value


def to_paths(blocks):
    return lax.all_to_all(blocks, "path", 0, 0, tiled=True)


def pick_kernel(picks, master, out):
    out[...] = master[...].astype(bf16)


def pick_modules(master, picks):
    mods, rows, columns = master.shape
    count = picks.shape[0]
    return pl.pallas_call(
        pick_kernel,
        out_shape=jax.ShapeDtypeStruct((count, rows, columns), bf16),
        grid_spec=pltpu.PrefetchScalarGridSpec(
            num_scalar_prefetch=1,
            grid=(count,),
            in_specs=[pl.BlockSpec((1, rows, columns), lambda i, picks: (picks[i], 0, 0))],
            out_specs=pl.BlockSpec((1, rows, columns), lambda i, picks: (i, 0, 0)),
        ),
        cost_estimate=pl.CostEstimate(
            flops=0, bytes_accessed=count * rows * columns * 6, transcendentals=0
        ),
    )(picks, master)


UNROLL = 16


def lookup_kernel(ids, table, out):
    base = pl.program_id(0) * out.shape[0]

    def step(i, carry):
        for j in range(UNROLL):
            row = ids[base + i * UNROLL + j]
            out[pl.ds(i * UNROLL + j, 1), :] = table[pl.ds(row, 1), :]
        return carry

    lax.fori_loop(0, out.shape[0] // UNROLL, step, 0)


def lookup(ids, table, block):
    count = ids.shape[0]
    rows, columns = table.shape
    return pl.pallas_call(
        lookup_kernel,
        out_shape=jax.ShapeDtypeStruct((count, columns), f32),
        grid_spec=pltpu.PrefetchScalarGridSpec(
            num_scalar_prefetch=1,
            grid=(count // block,),
            in_specs=[pl.BlockSpec((rows, columns), lambda i, ids: (0, 0))],
            out_specs=pl.BlockSpec((block, columns), lambda i, ids: (i, 0)),
        ),
        compiler_params=pltpu.CompilerParams(vmem_limit_bytes=40 << 20),
        cost_estimate=pl.CostEstimate(
            flops=count * 4096, bytes_accessed=(rows + count) * columns * 4, transcendentals=0
        ),
    )(ids, table)


def collect_kernel(ids, rows, out):
    base = pl.program_id(0) * rows.shape[0]

    @pl.when(pl.program_id(0) == 0)
    def clear():
        out[...] = jnp.zeros_like(out)

    def step(i, carry):
        for j in range(UNROLL):
            row = ids[base + i * UNROLL + j]
            out[pl.ds(row, 1), :] += rows[pl.ds(i * UNROLL + j, 1), :]
        return carry

    lax.fori_loop(0, rows.shape[0] // UNROLL, step, 0)


def collect(ids, rows, slots, block):
    count, columns = rows.shape
    return pl.pallas_call(
        collect_kernel,
        out_shape=jax.ShapeDtypeStruct((slots, columns), f32),
        grid_spec=pltpu.PrefetchScalarGridSpec(
            num_scalar_prefetch=1,
            grid=(count // block,),
            in_specs=[pl.BlockSpec((block, columns), lambda i, ids: (i, 0))],
            out_specs=pl.BlockSpec((slots, columns), lambda i, ids: (0, 0)),
        ),
        compiler_params=pltpu.CompilerParams(vmem_limit_bytes=40 << 20),
        cost_estimate=pl.CostEstimate(
            flops=count * 8192, bytes_accessed=(slots + count) * columns * 4, transcendentals=0
        ),
    )(ids, rows)


def adam_moments(first, second, gradient):
    first_new = beta_first * first.astype(f32) + (1.0 - beta_first) * gradient
    second_new = beta_second * second.astype(f32) + (1.0 - beta_second) * gradient * gradient
    update = (
        first_new
        / (1.0 - beta_first**step_count)
        / (jnp.sqrt(second_new / (1.0 - beta_second**step_count)) + adam_eps)
    )
    return (first_new, second_new, update)


def outer_step(master, momentum, average, decay, rate):
    outer_grad = rate * (average + decay * master)
    moment_new = outer_mu * momentum + outer_grad
    return (master - rate_outer * (outer_grad + outer_mu * moment_new), moment_new)


def module_means(incoming, shares):
    means = []
    for module in range(MODS):
        total = 0.0
        for path in range(incoming.shape[0]):
            total = total + shares[module, path] * incoming[path].astype(f32)
        means.append(total)
    return jnp.stack(means)


def body(
    token_ids,
    targets,
    loss_positions,
    doc_lengths,
    live_tokens,
    routes,
    attn_master,
    mlp_master,
    gain_master,
    table_master,
    attn_outer,
    mlp_outer,
    gain_outer,
    table_outer,
    attn_first,
    mlp_first,
    gain_first,
    table_first,
    attn_second,
    mlp_second,
    gain_second,
    table_second,
):
    paths = lax.axis_size("path")
    tp_count = lax.axis_size("tp")
    path_index = lax.axis_index("path")
    tp_index = lax.axis_index("tp")
    width = attn_first.shape[1]
    owned = attn_master.shape[1]
    seq_len = token_ids.shape[1]
    counted = loss_positions.shape[1]
    shard = seq_len // tp_count
    share = counted // tp_count
    vocab = table_master.shape[0]
    chunk = -(-vocab // (paths * LANES)) * LANES

    gain_low = gain_master.astype(bf16).astype(f32)
    gains_out = jnp.stack([gain_low[routes[:, 0], :, 0], gain_low[routes[:, 1], :, 1]], 1)
    own_small = jnp.concatenate(
        [
            token_ids[0].astype(f32),
            targets[0].astype(f32),
            jnp.broadcast_to(jnp.sum(live_tokens).astype(f32), (LANES,)),
        ]
    )
    small = to_paths(
        jnp.concatenate(
            [
                jnp.broadcast_to(own_small, (paths, own_small.shape[0])),
                gains_out.reshape(paths, 2 * owned),
            ],
            1,
        )
    )
    all_ids = small[:, :seq_len].astype(jnp.int32)
    all_targets = small[:, seq_len : seq_len + counted].astype(jnp.int32)
    counts = small[:, seq_len + counted]
    gains_in = small[:, seq_len + counted + LANES :].reshape(paths, 2, owned)
    gain_attn = gains_in[:, 0].reshape(width)
    gain_mlp = gains_in[:, 1].reshape(width)

    attn_w = to_paths(pick_modules(attn_master, routes[:, 0])).reshape(width, -1)

    table_t = table_master.T
    table_rows = jnp.pad(table_master, ((0, 8), (0, 0))).astype(bf16).astype(f32)
    local_ids = all_ids - tp_index * vocab
    local_ids = jnp.where((local_ids >= 0) & (local_ids < vocab), local_ids, vocab)
    looked = lookup(local_ids.reshape(-1), table_rows, seq_len)
    looked = looked.reshape(paths, tp_count, shard, owned).swapaxes(0, 1)
    looked = to_paths(tp_scatter(looked).astype(bf16))
    hidden_part = looked.swapaxes(0, 1).reshape(shard, width)
    hidden_low = tp_gather(hidden_part).reshape(seq_len, width)

    mlp_w = to_paths(pick_modules(mlp_master, routes[:, 1])).reshape(width, -1)

    table_out = jnp.pad(table_t.astype(bf16), ((0, 0), (0, paths * chunk - vocab)))
    table_out = table_out.reshape(owned, paths, chunk).swapaxes(0, 1)
    table_w = to_paths(table_out).reshape(width, chunk)

    slot_cols = attn_w.shape[1] // 4
    slots_here = slot_cols // HEAD_DIM
    missing = tp_count * slots_here - HEADS
    limit = slots_here - (tp_index >= tp_count - missing).astype(jnp.int32)
    validity = (jnp.arange(slots_here) < limit).astype(f32)
    validity = jnp.repeat(validity, HEAD_DIM)
    places = jnp.arange(seq_len, dtype=jnp.int32)
    positions = loss_positions[0]
    docs = doc_lengths.shape[1]
    ends = jnp.sum(
        jnp.where(jnp.arange(docs)[:, None] <= jnp.arange(docs)[None, :], doc_lengths[0][:, None], 0), 0
    )
    segments = jnp.sum((places[:, None] >= ends[None, :]).astype(jnp.int32), -1)
    seg_counted = jnp.sum((positions[:, None] >= ends[None, :]).astype(jnp.int32), -1)
    allowed = (seg_counted[:, None] == segments[None, :]) & (places[None, :] <= positions[:, None])
    chosen = (positions[:, None] == places[None, :]).astype(bf16)
    key_tables = angle_tables(places, slots_here)
    query_tables = angle_tables(positions, slots_here)

    hidden = hidden_low.astype(f32)
    normed_in = (normed(hidden) * gain_attn).astype(bf16)
    hidden_c = dot(chosen, hidden_low, ((1,), (0,)))
    normed_c = dot(chosen, normed_in, ((1,), (0,))).astype(bf16)
    queries = rotate(dot(normed_c, attn_w[:, :slot_cols], ((1,), (0,))), query_tables).astype(bf16)
    keys_values = dot(normed_in, attn_w[:, slot_cols : 3 * slot_cols], ((1,), (0,)))
    keys = rotate(keys_values[:, :slot_cols], key_tables).astype(bf16)
    values = keys_values[:, slot_cols:].astype(bf16)
    q_heads = queries.reshape(counted, slots_here, HEAD_DIM)
    k_heads = keys.reshape(seq_len, slots_here, HEAD_DIM)
    v_heads = values.reshape(seq_len, slots_here, HEAD_DIM)
    scale_factor = HEAD_DIM ** (-0.5)
    scores = jnp.einsum("qhe,khe->hqk", q_heads, k_heads, preferred_element_type=f32) * scale_factor
    scores = jnp.where(allowed[None], scores, -1e30)
    peak = jnp.max(scores, -1, keepdims=True)
    expo = jnp.exp(scores - peak)
    probs = expo / jnp.sum(expo, -1, keepdims=True)
    probs_low = probs.astype(bf16)
    mixed = jnp.einsum("hqk,khe->qhe", probs_low, v_heads, preferred_element_type=f32)
    mixed = (mixed.reshape(counted, slot_cols) * validity).astype(bf16)
    w_out = attn_w[:, 3 * slot_cols :]
    hidden_mid = hidden_c + tp_total(dot(mixed, w_out, ((1,), (1,))))
    normed_mid = (normed(hidden_mid) * gain_mlp).astype(bf16)
    hidden_cols = mlp_w.shape[1] // 2
    w_up, w_down = mlp_w[:, :hidden_cols], mlp_w[:, hidden_cols:]
    upward = dot(normed_mid, w_up, ((1,), (0,)))
    activ = jax.nn.gelu(upward, approximate=True).astype(bf16)
    mid_part = lax.dynamic_slice_in_dim(hidden_mid, tp_index * share, share, 0)
    final_part = mid_part + tp_scatter(
        dot(activ, w_down, ((1,), (1,))).reshape(tp_count, share, width)
    )
    head_part = normed(final_part).astype(bf16)

    heads = to_paths(jnp.broadcast_to(head_part, (paths,) + head_part.shape))
    head_in = tp_gather(heads).reshape(-1, width)
    total_rows = head_in.shape[0]
    logits = dot(head_in, table_w, ((1,), (0,)))
    entries = jnp.arange(chunk)
    here = jnp.minimum(vocab - path_index * chunk, chunk)
    logits = jnp.where(entries[None, :] < here, logits, -1e30)
    local_targets = all_targets.reshape(paths, tp_count, share).swapaxes(0, 1).reshape(-1)
    local_targets = local_targets - tp_index * vocab
    local_targets = jnp.where((local_targets >= 0) & (local_targets < vocab), local_targets, -1)
    local_targets = local_targets - path_index * chunk
    onehot = entries[None, :] == local_targets[:, None]
    top = jnp.max(logits, -1)
    expo_v = jnp.exp(logits - top[:, None])
    sums = jnp.sum(expo_v, -1)
    picked = jnp.sum(jnp.where(onehot, logits, 0.0), -1)
    best, total, hit = top, sums, picked
    for axis in ("tp", "path"):
        step = 1
        while step < lax.axis_size(axis):
            best_o, total_o, hit_o = swap(jnp.stack([best, total, hit]), axis, step)
            higher = jnp.maximum(best, best_o)
            total = total * jnp.exp(best - higher) + total_o * jnp.exp(best_o - higher)
            best, hit = higher, hit + hit_o
            step *= 2
    losses = (best + jnp.log(total) - hit).reshape(tp_count, paths, share)
    path_loss = jnp.sum(lax.dynamic_index_in_dim(losses, path_index, 1, keepdims=False)) / counted
    grad_logits = (
        (expo_v * (jnp.exp(top - best) / total)[:, None] - onehot.astype(f32)) / counted
    ).astype(bf16)
    grad_heads = dot(grad_logits, table_w, ((1,), (1,))).reshape(tp_count, paths, share, width)
    grad_head = jnp.sum(to_paths(tp_scatter(grad_heads).astype(bf16)).astype(f32), 0)
    head_grad = dot(head_in, grad_logits, ((0,), (0,))).astype(bf16)
    head_grad = to_paths(head_grad.reshape(paths, owned, chunk))
    head_grad = head_grad.swapaxes(0, 1).reshape(owned, paths * chunk)[:, :vocab].astype(f32)

    grad_final = norm_back(final_part, grad_head)
    grad_branch = tp_gather(grad_final.astype(bf16)).reshape(counted, width)
    down_grad = dot(grad_branch, activ, ((0,), (0,)))
    grad_activ = dot(grad_branch, w_down, ((1,), (0,)))
    unused, gelu_pull = jax.vjp(lambda inputs: jax.nn.gelu(inputs, approximate=True), upward)
    grad_up = gelu_pull(grad_activ)[0].astype(bf16)
    up_grad = dot(normed_mid, grad_up, ((0,), (0,)))
    grad_normed = tp_scatter(dot(grad_up, w_up, ((1,), (1,))).reshape(tp_count, share, width))
    gain_mlp_grad = jnp.sum(grad_normed * normed(mid_part), 0)
    grad_mid = grad_final + norm_back(mid_part, grad_normed * gain_mlp)
    grad_out = tp_gather(grad_mid.astype(bf16)).reshape(counted, width)
    out_grad = dot(grad_out, mixed, ((0,), (0,)))
    grad_mixed = (dot(grad_out, w_out, ((1,), (0,))) * validity).astype(bf16)
    g_heads = grad_mixed.reshape(counted, slots_here, HEAD_DIM)
    grad_probs = jnp.einsum("qhe,khe->hqk", g_heads, v_heads, preferred_element_type=f32)
    inner = jnp.sum(probs * grad_probs, -1, keepdims=True)
    grad_scores = (probs * (grad_probs - inner)).astype(bf16)
    grad_query = jnp.einsum("hqk,khe->qhe", grad_scores, k_heads, preferred_element_type=f32)
    grad_key = jnp.einsum("hqk,qhe->khe", grad_scores, q_heads, preferred_element_type=f32)
    grad_value = jnp.einsum("hqk,qhe->khe", probs_low, g_heads, preferred_element_type=f32)
    grad_query = grad_query.reshape(counted, slot_cols) * scale_factor
    grad_key = grad_key.reshape(seq_len, slot_cols) * scale_factor
    grad_query = rotate_back(grad_query, query_tables).astype(bf16)
    grad_kv = jnp.concatenate(
        [rotate_back(grad_key, key_tables), grad_value.reshape(seq_len, slot_cols)], 1
    ).astype(bf16)
    query_grad = dot(normed_c, grad_query, ((0,), (0,)))
    kv_grad = dot(normed_in, grad_kv, ((0,), (0,)))
    attn_grad = jnp.concatenate([query_grad, kv_grad, out_grad], 1)
    mlp_grad = jnp.concatenate([up_grad, down_grad], 1)
    grad_queries = dot(chosen, grad_query, ((0,), (0,))).astype(bf16)
    grad_proj = jnp.concatenate([grad_queries, grad_kv], 1)
    grad_in_part = dot(grad_proj, attn_w[:, : 3 * slot_cols], ((1,), (1,)))
    gain_attn_grad = jnp.sum(grad_in_part * normed(hidden), 0)

    squares = jnp.sum(attn_grad * attn_grad) + jnp.sum(mlp_grad * mlp_grad)
    joint = butterfly(
        jnp.concatenate([gain_attn_grad, gain_mlp_grad, jnp.broadcast_to(squares, (LANES,))]), "tp"
    )
    gain_grad = joint[: 2 * width].reshape(2, width).T
    path_norm = jnp.sqrt(joint[2 * width] + jnp.sum(gain_grad * gain_grad))
    factor = jnp.minimum(1.0, clip_limit / (path_norm + 1e-06))
    weight = lax.dynamic_index_in_dim(counts, path_index, 0, keepdims=False)

    m_first_new, m_second_new, m_update = adam_moments(mlp_first[0], mlp_second[0], mlp_grad * factor)
    m_in = to_paths((weight * m_update).astype(bf16).reshape(paths, owned, -1))
    a_first_new, a_second_new, a_update = adam_moments(
        attn_first[0], attn_second[0], attn_grad * factor
    )
    a_in = to_paths((weight * a_update).astype(bf16).reshape(paths, owned, -1))
    g_first_new, g_second_new, g_update = adam_moments(
        gain_first[0], gain_second[0], gain_grad * factor
    )
    g_in = to_paths((weight * g_update).T.reshape(2, paths, owned).swapaxes(0, 1))

    grad_in = tp_scatter(grad_in_part.reshape(tp_count, shard, width))
    own_hidden = hidden_part.astype(f32)
    chosen_part = lax.dynamic_slice_in_dim(chosen, tp_index * shard, shard, 1)
    grad_rows = dot(chosen_part, grad_out, ((0,), (0,))) + norm_back(own_hidden, grad_in * gain_attn)
    grad_rows = grad_rows.astype(bf16).reshape(shard, paths, owned).swapaxes(0, 1)
    grad_rows = tp_gather(to_paths(grad_rows)).reshape(-1, owned).astype(f32)
    row_ids = local_ids.reshape(paths, tp_count, shard).swapaxes(0, 1).reshape(-1)
    rows_total = collect(row_ids, grad_rows, vocab + 8, seq_len)
    table_grad = head_grad + rows_total[:vocab].T
    table_squares = jnp.broadcast_to(jnp.sum(table_grad * table_grad), (8, LANES))
    table_norm = jnp.sqrt(butterfly(butterfly(table_squares, "tp"), "path")[0, 0])
    table_clip = table_grad * jnp.minimum(1.0, clip_limit / (table_norm + 1e-06))
    t_first_new, t_second_new, t_update = adam_moments(table_first.T, table_second.T, table_clip)
    table_new, table_momentum = outer_step(table_t, table_outer.T, t_update, decay_rate, rate_inner)

    module_ids = jnp.arange(MODS)
    pick_attn = (routes[:, 0][None, :] == module_ids[:, None]).astype(f32)
    pick_mlp = (routes[:, 1][None, :] == module_ids[:, None]).astype(f32)
    share_attn = pick_attn / jnp.sum(pick_attn * counts[None, :], 1)[:, None]
    share_mlp = pick_mlp / jnp.sum(pick_mlp * counts[None, :], 1)[:, None]
    attn_new, attn_momentum = outer_step(
        attn_master, attn_outer, module_means(a_in, share_attn), decay_rate, rate_inner
    )
    mlp_new, mlp_momentum = outer_step(
        mlp_master, mlp_outer, module_means(m_in, share_mlp), decay_rate, rate_inner
    )
    gain_mean = jnp.stack(
        [
            jnp.sum(share_attn[:, :, None] * g_in[None, :, 0], 1),
            jnp.sum(share_mlp[:, :, None] * g_in[None, :, 1], 1),
        ],
        -1,
    )
    gain_new, gain_momentum = outer_step(gain_master, gain_outer, gain_mean, 0.0, rate_gain)
    return (
        attn_new,
        mlp_new,
        gain_new,
        table_new.T,
        attn_momentum,
        mlp_momentum,
        gain_momentum,
        table_momentum.T,
        a_first_new[None],
        m_first_new[None],
        g_first_new[None],
        t_first_new.T,
        a_second_new[None],
        m_second_new[None],
        g_second_new[None],
        t_second_new.T,
        path_loss[None],
        path_norm[None],
        table_norm,
    )


def solution(mesh):
    in_specs = (
        P("path", None),
        P("path", None),
        P("path", None),
        P("path", None),
        P("path"),
        P(),
        P(None, "path", "tp"),
        P(None, "path", "tp"),
        P(None, "path", None),
        P("tp", "path"),
        P(None, "path", "tp"),
        P(None, "path", "tp"),
        P(None, "path", None),
        P("tp", "path"),
        P("path", None, "tp"),
        P("path", None, "tp"),
        P("path", None, None),
        P("tp", "path"),
        P("path", None, "tp"),
        P("path", None, "tp"),
        P("path", None, None),
        P("tp", "path"),
    )
    out_specs = (
        P(None, "path", "tp"),
        P(None, "path", "tp"),
        P(None, "path", None),
        P("tp", "path"),
        P(None, "path", "tp"),
        P(None, "path", "tp"),
        P(None, "path", None),
        P("tp", "path"),
        P("path", None, "tp"),
        P("path", None, "tp"),
        P("path", None, None),
        P("tp", "path"),
        P("path", None, "tp"),
        P("path", None, "tp"),
        P("path", None, None),
        P("tp", "path"),
        P("path"),
        P("path"),
        P(),
    )
    return jax.shard_map(body, mesh=mesh, in_specs=in_specs, out_specs=out_specs, check_vma=False)
```

time: 1580 us -> 744 us (0.47)
  waiting for transfers between devices: 919 us -> 219 us
  blocking collectives: 113 us -> 0 us
  matrix products: 145 us -> 54.4 us
  starting transfers between devices: 15.6 us -> 87.1 us
  Pallas kernels: 0 us -> 69.4 us
  local copies, waits for them, and re-layouts: 167 us -> 121 us
  between operations: 27.6 us -> 10.9 us
    all_gather x3 -> x0, waiting for transfers between devices: 389 us -> none  [the longest x1 201 us: body(): lax.all_gather(table_master.astype(jnp.bfloat16), 'path', axis=1, tiled=T...]
    psum x6 -> x0, waiting for transfers between devices: 365 us -> none  [the longest x3 170 us: input_total(): return lax.psum(partial_grad, 'tp')]
    ppermute x0 -> x36, waiting for transfers between devices: none -> 96.7 us  [swap(): return lax.ppermute(value, axis, [(i, i ^ step) for i in range(count)])]
    dot_general x33 -> x26, matrix products: 145 us -> 51.1 us  [the longest x21 44.5 us: dot(): lax.dot_general(left, right, (dims, ((), ())), preferred_element_type=f32)]
    pallas_call x0 -> x4, Pallas kernels: none -> 69.4 us  [the longest x1 45.6 us: collect(): pl.pallas_call(collect_kernel, out_shape=jax.ShapeDtypeStruct((slots, col...]
    unnamed x11 -> x0, waiting for transfers between devices: 61 us -> none
    psum x3 -> x0, blocking collectives: 51.7 us -> none  [the longest x1 39.5 us: body(): lax.psum(jnp.sum(table_part * table_part), ('path', 'tp'))]
    add x9 -> x23, other arithmetic: 24.8 us -> 76.2 us  [the longest x8 50.4 us: module_means(): total = total + shares[module, path] * incoming[path].astype(f32)]
  transfers between devices with their start and end apart: 13 -> 48, of which waited for: 12 -> 32; matrix products, arithmetic and copies ran while one was open for 12% -> 33% of each run, Pallas kernels for 0% -> 8%
where the time goes in v1:
time: 744 us; the launch traced here: 734 us
  waiting for transfers between devices  219 us (29%)
  other arithmetic  173 us (23%)
  local copies, waits for them, and re-layouts  121 us (16%)
  starting transfers between devices  87.1 us (12%)
  Pallas kernels  69.4 us (9%)
  matrix products  54.4 us (7%)
  between operations  10.9 us (1%)
    all_to_all x12, waiting for transfers between devices, to_paths(): return lax.all_to_all(blocks, 'path', 0, 0, tiled=True)  122 us
    ppermute x36, waiting for transfers between devices, swap(): return lax.ppermute(value, axis, [(i, i ^ step) for i in range(count)])  96.7 us
    all_to_all x12, starting transfers between devices, to_paths(): return lax.all_to_all(blocks, 'path', 0, 0, tiled=True)  56.9 us
    add x8, other arithmetic, module_means(): total = total + shares[module, path] * incoming[path].astype(f32)  50.4 us
    unnamed x192, local copies, waits for them, and re-layouts  50 us
    pallas_call x1, Pallas kernels, collect(): pl.pallas_call(collect_kernel, out_shape=jax.ShapeDtypeStruct((slots, col...  45.6 us
    dot_general x21, matrix products, dot(): lax.dot_general(left, right, (dims, ((), ())), preferred_element_type=f32)  44.5 us
    ppermute x36, starting transfers between devices, swap(): return lax.ppermute(value, axis, [(i, i ^ step) for i in range(count)])  30.2 us
  transfers between devices with their start and end apart: 48, of which 32 were waited for; matrix products, arithmetic and copies ran while one was open for 33% of the time, Pallas kernels for 8%

profile of v1, /device:TPU:0, one launch (start us, length us, event | category | flops | bytes accessed | tf_op | source)
XLA Modules:
  0.0 734.4 jit_solution(14435539793906503374)
XLA Ops:
  6.6 7.3 all-to-all-start
  24.8 9.8 %shard_map.357 = f32[8192,112]{1,0:T(8,128)S(1)} custom-call(s32[8192]{0:T(1024)S(1)} %bitcast.470, f32[8008,112]{1,0:T(8,128)S(1)} %copy-done.3), custom_call_target="tpu_custom_call" | custom-call | flops 33554432 | bytes 7257600 | tf_op jit(solution)/shard_map/pallas_call | solution.py:163
  36.7 5.3 copy.282
  49.4 11.1 %collective-permute-done.1 = bf16[1,8,256,112]{2,3,1,0:T(8,128)(2,1)S(1)} collective-permute-done((bf16[1,8,256,112]{2,3,1,0:T(8,128)(2,1)S(1)}, bf16[1,8,256,112]{2,3,1,0:T(8,128)(2,1)S(1)}, u32[]{:S(2)}, u32[]{:S(2)}) %collective-permute-start.1) | collective-permute-done | bytes 458784 | tf_op jit(solution)/shard_map/ppermute | solution.py:72
  61.4 6.0 all-to-all-start.1
  67.4 6.3 shard_map.358
  73.6 6.3 all-to-all-done.1
  88.4 7.7 %shard_map.359 = bf16[8,112,1792]{2,1,0:T(8,128)(2,1)} custom-call(s32[8]{0:T(128)} %get-tuple-element.365.picks, f32[4,112,1792]{2,1,0:T(8,128)} %master.3), custom_call_target="tpu_custom_call" | custom-call | bytes 9633792 | tf_op jit(solution)/shard_map/pallas_call | solution.py:130
  103.0 22.8 %all-to-all-done.2 = bf16[8,112,1024]{2,1,0:T(8,128)(2,1)} async-done(((bf16[8,112,1024]{2,1,0:T(8,128)(2,1)}), bf16[8,112,1024]{2,1,0:T(8,128)(2,1)}, u32[]{:S(2)}, u32[]{:S(2)}) %all-to-all-start.2) | async-done | bytes 1835040 | tf_op jit(solution)/shard_map/all_to_all | solution.py:120
  125.8 4.6 all-to-all-start.3
  164.7 37.2 %all-to-all-done.3 = bf16[8,112,1792]{2,1,0:T(8,128)(2,1)} async-done(((bf16[8,112,1792]{2,1,0:T(8,128)(2,1)}), bf16[8,112,1792]{2,1,0:T(8,128)(2,1)}, u32[]{:S(2)}, u32[]{:S(2)}) %all-to-all-start.3) | async-done | bytes 3211296 | tf_op jit(solution)/shard_map/all_to_all | solution.py:120
  209.6 5.4 copy.295
  225.5 7.9 %all-to-all-done.4 = bf16[8,32,896]{2,1,0:T(8,128)(2,1)S(1)} async-done(((bf16[8,32,896]{2,1,0:T(8,128)(2,1)}), bf16[8,32,896]{2,1,0:T(8,128)(2,1)S(1)}, u32[]{:S(2)}, u32[]{:S(2)}) %all-to-all-start.4) | async-done | bytes 458784 | tf_op jit(solution)/shard_map/all_to_all | solution.py:120
  233.3 4.5 all-to-all-start.5
  238.5 10.9 %collective-permute-done.10 = bf16[8,32,896]{2,1,0:T(8,128)(2,1)S(1)} collective-permute-done((bf16[8,32,896]{2,1,0:T(8,128)(2,1)S(1)}, bf16[8,32,896]{2,1,0:T(8,128)(2,1)S(1)}, u32[]{:S(2)}, u32[]{:S(2)}) %collective-permute-start.10) | collective-permute-done | bytes 458784 | tf_op jit(solution)/shard_map/ppermute | solution.py:72
  255.1 25.0 %all-to-all-done.5 = bf16[8,112,1024]{2,1,0:T(8,128)(2,1)} async-done(((bf16[8,112,1024]{2,1,0:T(8,128)(2,1)}), bf16[8,112,1024]{2,1,0:T(8,128)(2,1)}, u32[]{:S(2)}, u32[]{:S(2)}) %all-to-all-start.5) | async-done | bytes 1835040 | tf_op jit(solution)/shard_map/all_to_all | solution.py:120
  280.0 4.5 select_reduce_fusion.1
  300.8 4.4 collective-permute-done.16
  307.6 4.6 fusion.218
  315.7 5.4 copy.313
  339.4 8.9 %all-to-all-done.6 = bf16[8,32,896]{2,1,0:T(8,128)(2,1)S(1)} async-done(((bf16[8,32,896]{2,1,0:T(8,128)(2,1)}), bf16[8,32,896]{2,1,0:T(8,128)(2,1)S(1)}, u32[]{:S(2)}, u32[]{:S(2)}) %all-to-all-start.6) | async-done | bytes 458784 | tf_op jit(solution)/shard_map/all_to_all | solution.py:120
  392.2 4.8 multiply_reduce_fusion.1
  449.0 5.5 convolution_convert_fusion
  462.7 7.0 fusion.22
  469.8 11.5 %fusion.7 = (f32[1,896,1792]{2,1,0:T(8,128)}, f32[1,896,1792]{2,1,0:T(8,128)}, f32[1,896,1792]{2,1,0:T(8,128)}, f32[1,896,1792]{2,1,0:T(8,128)}) fusion(f32[1,896,896]{2,1,0:T(8,128)S(1)} %bitcast.474, f32[1,896,896]{2,1,0:T(8,128)S(1)} %bitcast.471, f32[]{:T(128)S(6)} %min.10, bf16[1,896,1792]{2,1,0:T(8,128)(2,1)} %param.41, bf16[1,896,1792]{2,1,0:T(8,128)(2,1)} %param.37), kind=kLoop, calls=%fused_computation.11 | loop fusion | flops 17661952 | bytes 38535172 | tf_op jit(solution)/shard_map/add | solution.py:215
  481.9 5.6 fusion.24
  487.5 4.7 collective-permute-done.29
  494.2 10.1 %all-to-all-done.10 = bf16[8,112,1024]{2,1,0:T(8,128)(2,1)} async-done(((bf16[8,112,1024]{2,1,0:T(8,128)(2,1)}), bf16[8,112,1024]{2,1,0:T(8,128)(2,1)}, u32[]{:S(2)}, u32[]{:S(2)}) %all-to-all-start.10) | async-done | bytes 1835040 | tf_op jit(solution)/shard_map/all_to_all | solution.py:120
  504.2 4.3 all-to-all-start.7
  510.7 9.6 %fusion.9 = bf16[8,112,1792]{2,1,0:T(8,128)(2,1)} fusion(f32[8,112,1792]{2,1,0:T(8,128)} %bitcast.476, f32[8,112,1792]{2,1,0:T(8,128)} %bitcast.475, f32[8,112,896]{2,1,0:T(8,128)} %bitcast.473, f32[8,112,896]{2,1,0:T(8,128)S(1)} %bitcast.472, f32[]{:T(128)S(6)} %min.10, f32[]{:T(128)} %bitcast.9), kind=kLoop, calls=%fused_computation.19 | loop fusion | flops 20873216 | bytes 22478856 | tf_op jit(solution)/shard_map/convert_element_type | solution.py:453
  528.9 5.2 copy.311
  536.3 45.6 %shard_map.360 = f32[8008,112]{1,0:T(8,128)S(1)} custom-call(s32[8192]{0:T(1024)S(1)} %bitcast.469, f32[8192,112]{1,0:T(8,128)S(1)} %bitcast.468), custom_call_target="tpu_custom_call" | custom-call | flops 67108864 | bytes 7257600 | tf_op jit(solution)/shard_map/pallas_call | solution.py:197
  586.2 6.2 all-to-all-start.8
  592.4 6.9 fusion.108
  602.3 7.2 fusion.115
  612.2 6.7 fusion.122
  620.9 7.0 fusion.129
  627.9 18.3 %collective-permute-done.34 = f32[8,128]{1,0:T(8,128)S(1)} collective-permute-done((f32[8,128]{1,0:T(8,128)S(1)}, f32[8,128]{1,0:T(8,128)S(1)}, u32[]{:S(2)}, u32[]{:S(2)}) %collective-permute-start.34) | collective-permute-done | bytes 4128 | tf_op jit(solution)/shard_map/ppermute | solution.py:72
  652.5 12.8 %collective-permute-done.35 = f32[8,128]{1,0:T(8,128)S(1)} collective-permute-done((f32[8,128]{1,0:T(8,128)S(1)}, f32[8,128]{1,0:T(8,128)S(1)}, u32[]{:S(2)}, u32[]{:S(2)}) %collective-permute-start.35) | collective-permute-done | bytes 4128 | tf_op jit(solution)/shard_map/ppermute | solution.py:72
  666.5 13.7 %fusion.25 = (f32[8000,112]{1,0:T(8,128)}, f32[112,8000]{0,1:T(8,128)S(1)}, f32[8000,112]{1,0:T(8,128)}, f32[8000,112]{1,0:T(8,128)}) fusion(f32[8000,112]{1,0:T(8,128)} %copy.313, f32[8000,112]{1,0:T(8,128)} %copy.295, f32[8000,112]{1,0:T(8,128)} %copy.312, f32[]{:T(128)S(6)} %min.11, f32[8008,112]{1,0:T(8,128)} %copy-done, bf16[112,8192]{0,1:T(8,128)(2,1)} %bitcast.478, ...), kind=kLoop, calls=%fused_computation.59 | loop fusion | flops 17024000 | bytes 34048004 | tf_op jit(solution)/shard_map/transpose | solution.py:505
  683.1 5.4 copy.316
  688.5 5.4 copy.318
  694.0 5.4 copy.319
  699.4 5.4 copy.320
  704.8 5.5 fusion.70
  710.3 5.5 fusion.77
  715.8 6.2 fusion.84
  722.0 5.4 fusion.91
  (505 shorter events, 280.6 us)
Async XLA Ops:
  6.6 16.1 %all-to-all-start = ((f32[8,1,1504]{2,1,0:T(1,128)}), f32[8,1,1504]{2,1,0:T(1,128)S(1)}, u32[]{:S(2)}, u32[]{:S(2)}) async-start(f32[8,1,1504]{2,1,0:T(1,128)} %all_to_all.41), calls=%async_computation | async-start | bytes 98304 | tf_op jit(solution)/shard_map/all_to_all | solution.py:120
  43.6 2.5 collective-permute-start
  47.9 12.6 %collective-permute-start.1 = (bf16[1,8,256,112]{2,3,1,0:T(8,128)(2,1)S(1)}, bf16[1,8,256,112]{2,3,1,0:T(8,128)(2,1)S(1)}, u32[]{:S(2)}, u32[]{:S(2)}) collective-permute-start(bf16[1,8,256,112]{2,3,1,0:T(8,128)(2,1)S(1)} %dynamic-slice_convert_fusion.4), channel_id=1, source_target_pairs={{0,2},{1,3},{2,0},{3,1},{4,6},{5,7},{6,4},{7,5},{8,10},{9,11},{10,... | collective-permute-start | bytes 1376264 | tf_op jit(solution)/shard_map/ppermute | solution.py:72
  61.4 18.6 %all-to-all-start.1 = ((bf16[8,256,112]{1,2,0:T(8,128)(2,1)}), bf16[8,256,112]{1,2,0:T(8,128)(2,1)S(1)}, u32[]{:S(2)}, u32[]{:S(2)}) async-start(bf16[8,256,112]{1,2,0:T(8,128)(2,1)} %fusion.130), calls=%async_computation.1 | async-start | bytes 917504 | tf_op jit(solution)/shard_map/all_to_all | solution.py:120
  80.0 45.8 %all-to-all-start.2 = ((bf16[8,112,1024]{2,1,0:T(8,128)(2,1)}), bf16[8,112,1024]{2,1,0:T(8,128)(2,1)}, u32[]{:S(2)}, u32[]{:S(2)}) async-start(bf16[8,112,1024]{2,1,0:T(8,128)(2,1)} %shard_map.358), calls=%async_computation.2 | async-start | bytes 3670016 | tf_op jit(solution)/shard_map/all_to_all | solution.py:120
  84.3 12.0 %collective-permute-start.2 = (bf16[256,896]{0,1:T(8,128)(2,1)S(1)}, bf16[256,896]{0,1:T(8,128)(2,1)S(1)}, u32[]{:S(2)}, u32[]{:S(2)}) collective-permute-start(bf16[256,896]{0,1:T(8,128)(2,1)S(1)} %bitcast.493), channel_id=1, source_target_pairs={{0,2},{1,3},{2,0},{3,1},{4,6},{5,7},{6,4},{7,5},{8,10},{9,11},{10,... | collective-permute-start | bytes 1376264 | tf_op jit(solution)/shard_map/ppermute | solution.py:72
  96.5 3.7 collective-permute-start.3
  125.8 76.1 %all-to-all-start.3 = ((bf16[8,112,1792]{2,1,0:T(8,128)(2,1)}), bf16[8,112,1792]{2,1,0:T(8,128)(2,1)}, u32[]{:S(2)}, u32[]{:S(2)}) async-start(bf16[8,112,1792]{2,1,0:T(8,128)(2,1)} %shard_map.359), calls=%async_computation.3 | async-start | bytes 6422528 | tf_op jit(solution)/shard_map/all_to_all | solution.py:120
  152.6 1.4 collective-permute-start.4
  154.0 4.2 collective-permute-start.5
  158.3 4.2 collective-permute-start.6
  162.6 1.4 collective-permute-start.7
  206.6 1.4 collective-permute-start.8
  208.0 6.9 collective-permute-start.9
  216.5 16.8 %all-to-all-start.4 = ((bf16[8,32,896]{2,1,0:T(8,128)(2,1)}), bf16[8,32,896]{2,1,0:T(8,128)(2,1)S(1)}, u32[]{:S(2)}, u32[]{:S(2)}) async-start(bf16[8,32,896]{2,1,0:T(8,128)(2,1)} %broadcast_in_dim.77), calls=%async_computation.4 | async-start | bytes 917504 | tf_op jit(solution)/shard_map/all_to_all | solution.py:120
  233.3 46.7 %all-to-all-start.5 = ((bf16[8,112,1024]{2,1,0:T(8,128)(2,1)}), bf16[8,112,1024]{2,1,0:T(8,128)(2,1)}, u32[]{:S(2)}, u32[]{:S(2)}) async-start(bf16[8,112,1024]{2,1,0:T(8,128)(2,1)} %bitcast.492), calls=%async_computation.5 | async-start | bytes 3670016 | tf_op jit(solution)/shard_map/all_to_all | solution.py:120
  237.9 11.5 %collective-permute-start.10 = (bf16[8,32,896]{2,1,0:T(8,128)(2,1)S(1)}, bf16[8,32,896]{2,1,0:T(8,128)(2,1)S(1)}, u32[]{:S(2)}, u32[]{:S(2)}) collective-permute-start(bf16[8,32,896]{2,1,0:T(8,128)(2,1)S(1)} %all-to-all-done.4), channel_id=1, source_target_pairs={{0,2},{1,3},{2,0},{3,1},{4,6},{5,7},{6,4},{7,5},{8,10},{9,11},{10,... | collective-permute-start | bytes 1376264 | tf_op jit(solution)/shard_map/ppermute | solution.py:72
  249.6 2.7 collective-permute-start.11
  286.4 1.2 collective-permute-start.12
  287.7 3.8 collective-permute-start.13
  291.6 3.8 collective-permute-start.14
  296.1 3.8 collective-permute-start.15
  300.5 4.7 collective-permute-start.16
  312.3 2.5 collective-permute-start.17
  315.1 14.5 %collective-permute-start.18 = (bf16[1,8,32,896]{3,2,1,0:T(8,128)(2,1)S(1)}, bf16[1,8,32,896]{3,2,1,0:T(8,128)(2,1)}, u32[]{:S(2)}, u32[]{:S(2)}) collective-permute-start(bf16[1,8,32,896]{3,2,1,0:T(8,128)(2,1)S(1)} %dynamic-slice_convert_fusion.3), channel_id=1, source_target_pairs={{0,2},{1,3},{2,0},{3,1},{4,6},{5,7},{6,4},{7,5},{8,10},{9,11},{10,... | collective-permute-start | bytes 1376264 | tf_op jit(solution)/shard_map/ppermute | solution.py:72
  331.5 16.8 %all-to-all-start.6 = ((bf16[8,32,896]{2,1,0:T(8,128)(2,1)}), bf16[8,32,896]{2,1,0:T(8,128)(2,1)S(1)}, u32[]{:S(2)}, u32[]{:S(2)}) async-start(bf16[8,32,896]{2,1,0:T(8,128)(2,1)} %fusion.131), calls=%async_computation.6 | async-start | bytes 917504 | tf_op jit(solution)/shard_map/all_to_all | solution.py:120
  348.7 4.2 collective-permute-start.19
  353.0 1.4 collective-permute-start.20
  358.8 6.9 collective-permute-start.21
  365.8 4.3 collective-permute-start.22
  372.7 4.2 collective-permute-start.23
  377.0 2.3 collective-permute-start.24
  398.0 20.9 %collective-permute-start.27 = (bf16[2,256,896]{2,1,0:T(8,128)(2,1)}, bf16[2,256,896]{2,1,0:T(8,128)(2,1)}, u32[]{:S(2)}, u32[]{:S(2)}) collective-permute-start(bf16[2,256,896]{2,1,0:T(8,128)(2,1)} %fusion.60), channel_id=1, source_target_pairs={{0,1},{1,0},{2,3},{3,2},{4,5},{5,4},{6,7},{7,6},{8,9},{9,8},{10,11... | collective-permute-start | bytes 2752520 | tf_op jit(solution)/shard_map/ppermute | solution.py:72
  405.2 5.2 collective-permute-start.25
  411.7 6.4 collective-permute-start.26
  422.9 12.5 %collective-permute-start.28 = (bf16[1,256,896]{2,1,0:T(8,128)(2,1)}, bf16[1,256,896]{2,1,0:T(8,128)(2,1)}, u32[]{:S(2)}, u32[]{:S(2)}) collective-permute-start(bf16[1,256,896]{2,1,0:T(8,128)(2,1)} %dynamic-slice_convert_fusion.2), channel_id=1, source_target_pairs={{0,2},{1,3},{2,0},{3,1},{4,6},{5,7},{6,4},{7,5},{8,10},{9,11},{10,... | collective-permute-start | bytes 1376264 | tf_op jit(solution)/shard_map/ppermute | solution.py:72
  428.6 13.2 %all-to-all-start.9 = ((f32[8,2,112]{2,1,0:T(2,128)}), f32[8,2,112]{2,1,0:T(2,128)S(1)}, u32[]{:S(2)}, u32[]{:S(2)}) async-start(f32[8,2,112]{2,1,0:T(2,128)} %copy.302), calls=%async_computation.9 | async-start | bytes 16384 | tf_op jit(solution)/shard_map/all_to_all | solution.py:120
  441.9 16.5 %all-to-all-start.11 = ((bf16[8,256,112]{1,2,0:T(8,128)(2,1)}), bf16[8,256,112]{1,2,0:T(8,128)(2,1)}, u32[]{:S(2)}, u32[]{:S(2)}) async-start(bf16[8,256,112]{1,2,0:T(8,128)(2,1)} %bitcast.508), calls=%async_computation.11 | async-start | bytes 917504 | tf_op jit(solution)/shard_map/all_to_all | solution.py:120
  458.4 45.8 %all-to-all-start.10 = ((bf16[8,112,1024]{2,1,0:T(8,128)(2,1)}), bf16[8,112,1024]{2,1,0:T(8,128)(2,1)}, u32[]{:S(2)}, u32[]{:S(2)}) async-start(bf16[8,112,1024]{2,1,0:T(8,128)(2,1)} %bitcast.507), calls=%async_computation.10 | async-start | bytes 3670016 | tf_op jit(solution)/shard_map/all_to_all | solution.py:120
  481.3 10.9 %collective-permute-start.29 = (bf16[8,256,112]{1,2,0:T(8,128)(2,1)}, bf16[8,256,112]{1,2,0:T(8,128)(2,1)S(1)}, u32[]{:S(2)}, u32[]{:S(2)}) collective-permute-start(bf16[8,256,112]{1,2,0:T(8,128)(2,1)} %all-to-all-done.11), channel_id=1, source_target_pairs={{0,2},{1,3},{2,0},{3,1},{4,6},{5,7},{6,4},{7,5},{8,10},{9,11},{10,... | collective-permute-start | bytes 1376264 | tf_op jit(solution)/shard_map/ppermute | solution.py:72
  504.2 82.0 %all-to-all-start.7 = ((bf16[8,112,1024]{2,1,0:T(8,128)(2,1)}), bf16[8,112,1024]{2,1,0:T(8,128)(2,1)}, u32[]{:S(2)}, u32[]{:S(2)}) async-start(bf16[8,112,1024]{2,1,0:T(8,128)(2,1)} %fusion.24), calls=%async_computation.7 | async-start | bytes 3670016 | tf_op jit(solution)/shard_map/all_to_all | solution.py:120
  510.7 14.0 %collective-permute-start.30 = (bf16[2,8,256,112]{2,3,1,0:T(8,128)(2,1)}, bf16[2,8,256,112]{2,3,1,0:T(8,128)(2,1)}, u32[]{:S(2)}, u32[]{:S(2)}) collective-permute-start(bf16[2,8,256,112]{2,3,1,0:T(8,128)(2,1)} %pad_maximum_fusion.6), channel_id=1, source_target_pairs={{0,1},{1,0},{2,3},{3,2},{4,5},{5,4},{6,7},{7,6},{8,9},{9,8},{10,11... | collective-permute-start | bytes 2752520 | tf_op jit(solution)/shard_map/ppermute | solution.py:72
  586.1 13.2 %collective-permute-start.31 = (f32[8,128]{1,0:T(8,128)S(1)}, f32[8,128]{1,0:T(8,128)S(1)}, u32[]{:S(2)}, u32[]{:S(2)}) collective-permute-start(f32[8,128]{1,0:T(8,128)S(1)} %broadcast_in_dim.82), channel_id=1, source_target_pairs={{0,1},{1,0},{2,3},{3,2},{4,5},{5,4},{6,7},{7,6},{8,9},{9,8},{10,11... | collective-permute-start | bytes 12296 | tf_op jit(solution)/shard_map/ppermute | solution.py:72
  586.2 118.6 %all-to-all-start.8 = ((bf16[8,112,1792]{2,1,0:T(8,128)(2,1)}), bf16[8,112,1792]{2,1,0:T(8,128)(2,1)S(1)}, u32[]{:S(2)}, u32[]{:S(2)}) async-start(bf16[8,112,1792]{2,1,0:T(8,128)(2,1)} %fusion.9), calls=%async_computation.8 | async-start | bytes 6422528 | tf_op jit(solution)/shard_map/all_to_all | solution.py:120
  600.0 9.5 %collective-permute-start.32 = (f32[8,128]{1,0:T(8,128)S(1)}, f32[8,128]{1,0:T(8,128)S(1)}, u32[]{:S(2)}, u32[]{:S(2)}) collective-permute-start(f32[8,128]{1,0:T(8,128)S(1)} %broadcast_add_fusion), channel_id=1, source_target_pairs={{0,2},{1,3},{2,0},{3,1},{4,6},{5,7},{6,4},{7,5},{8,10},{9,11},{10,... | collective-permute-start | bytes 12296 | tf_op jit(solution)/shard_map/ppermute | solution.py:72
  610.1 9.0 %collective-permute-start.33 = (f32[8,128]{1,0:T(8,128)S(1)}, f32[8,128]{1,0:T(8,128)S(1)}, u32[]{:S(2)}, u32[]{:S(2)}) collective-permute-start(f32[8,128]{1,0:T(8,128)S(1)} %fusion.253), channel_id=1, source_target_pairs={{0,4},{4,0},{8,12},{12,8},{16,20},{20,16},{24,28},{28,24},{1,5},{5... | collective-permute-start | bytes 12296 | tf_op jit(solution)/shard_map/ppermute | solution.py:72
  619.1 27.1 %collective-permute-start.34 = (f32[8,128]{1,0:T(8,128)S(1)}, f32[8,128]{1,0:T(8,128)S(1)}, u32[]{:S(2)}, u32[]{:S(2)}) collective-permute-start(f32[8,128]{1,0:T(8,128)S(1)} %add.806), channel_id=1, source_target_pairs={{0,8},{4,12},{8,0},{12,4},{16,24},{20,28},{24,16},{28,20},{1,9},{5... | collective-permute-start | bytes 12296 | tf_op jit(solution)/shard_map/ppermute | solution.py:72
  646.2 19.1 %collective-permute-start.35 = (f32[8,128]{1,0:T(8,128)S(1)}, f32[8,128]{1,0:T(8,128)S(1)}, u32[]{:S(2)}, u32[]{:S(2)}) collective-permute-start(f32[8,128]{1,0:T(8,128)S(1)} %add.807), channel_id=1, source_target_pairs={{0,16},{4,20},{8,24},{12,28},{16,0},{20,4},{24,8},{28,12},{1,17},{... | collective-permute-start | bytes 12296 | tf_op jit(solution)/shard_map/ppermute | solution.py:72
  (90 other events, 1066.4 us)
